TPU v7x, 128 devices: a whole 4x4x4 slice. The times are simulated.
128 devices in a mesh: shard: 8 (over x, core), owner: 16 (over z, y).
Axes of the slice: x: 4, y: 4, z: 4, core: 2. Of those that a mesh axis runs over, the one named last changes fastest.
Arguments:
- gradient: float32 [128, 2048, 768], P('owner', 'shard'), may hold values from -6 to 6
- old_basis: float32 [128, 2048, 256], P('owner', 'shard'), may hold values from -0.125 to 0.125
- moment_one: float32 [128, 256, 768], P('owner', 'shard'), may hold values from -6 to 6
- moment_two: float32 [128, 256, 768], P('owner', 'shard'), may hold values from 0.01 to 1
- slot_expert: int32 [128], replicated, may hold values from 0 to 127, as said below
- cost: int32 [128], replicated, may hold values from 0 to 5
Outputs:
- new_basis: float32 [128, 2048, 256], P('owner', 'shard')
- new_moment_one: float32 [128, 256, 768], P('owner', 'shard')
- new_moment_two: float32 [128, 256, 768], P('owner', 'shard')
- update: bfloat16 [128, 2048, 768], P('owner', 'shard')
Inputs may be any that keep to these rules, and one draw needn't show every extreme that they name: `slot_expert`: A permutation of the 128 experts. Expert e's gradient lies in owner group e // 8; state slot s lies in owner group s // 8. The 8 slots of one owner group hold experts of 8 different owner groups, and the 8 experts of one owner group are held by 8 different owner groups.
All inputs are finite; a program needn't handle non-finite values.
Results may differ from a plain program's by a relative error of at most 0.001.
Values sent between devices are 32-bit elements; how exact they have to be, the bound alone decides.
A program may use at most 192 MiB of HBM per device.

v0:
```python
import jax
import jax.numpy as jnp
from jax import lax
from jax.sharding import PartitionSpec as P

HIGHEST_PREC = lax.Precision.HIGHEST
BETA_ONE = 0.9
BETA_TWO = 0.99
EPSILON = 1e-08
GALORE_SCALE = 0.25


def whole_step(basis_now, grad_now):
    inner_prod = jnp.dot(grad_now.T, basis_now, precision=HIGHEST_PREC)
    tall_block = jnp.dot(grad_now, inner_prod, precision=HIGHEST_PREC)
    gram_matrix = jnp.dot(tall_block.T, tall_block, precision=HIGHEST_PREC)
    factor = jnp.linalg.cholesky(gram_matrix)
    return lax.linalg.triangular_solve(
        factor, tall_block, left_side=False, lower=True, transpose_a=True
    )


def refresh_project(grad_slices, basis_slices, counts):
    slots = grad_slices.shape[0]
    grad_whole, basis_whole = (
        lax.all_to_all(grad_slices, "shard", split_axis=0, concat_axis=1, tiled=True),
        lax.all_to_all(basis_slices, "shard", split_axis=0, concat_axis=1, tiled=True),
    )
    shard_now = lax.axis_index("shard")
    my_count = jnp.sum(jnp.where(jnp.arange(slots) == shard_now, counts, 0))
    grad_now = grad_whole[0]
    basis_new = lax.fori_loop(
        0, my_count, lambda step_index, current: whole_step(current, grad_now), basis_whole[0]
    )
    projected = jnp.dot(basis_new.T, grad_now, precision=HIGHEST_PREC)
    basis_back, proj_back = (
        lax.all_to_all(basis_new[None], "shard", split_axis=1, concat_axis=0, tiled=True),
        lax.all_to_all(projected[None], "shard", split_axis=1, concat_axis=0, tiled=True),
    )
    return (basis_back, proj_back)


def on_device(gradient, old_basis, moment_one, moment_two, slot_expert, cost):
    slots = gradient.shape[0]
    owners = lax.axis_size("owner")
    owner_now = lax.axis_index("owner")
    table = slot_expert.reshape(owners, slots)
    mine = lax.dynamic_index_in_dim(table, owner_now, 0, keepdims=False)
    home_pick = (mine[:, None] // slots == jnp.arange(owners)[None, :]).astype(jnp.float32)
    own_ids = owner_now * slots + jnp.arange(slots)
    send_pick = jnp.sum((table[:, :, None] == own_ids[None, None, :]).astype(jnp.float32), axis=1)
    slot_counts = jnp.sum(
        jnp.where(mine[:, None] == jnp.arange(cost.shape[0])[None, :], cost[None, :], 0), axis=1
    )
    outgoing = jnp.einsum("oi,irc->orc", send_pick, gradient, precision=HIGHEST_PREC)
    arrived = lax.all_to_all(outgoing, "owner", split_axis=0, concat_axis=0, tiled=True)
    slot_grad = jnp.einsum("jh,hrc->jrc", home_pick, arrived, precision=HIGHEST_PREC)
    basis_slot, projected = refresh_project(slot_grad, old_basis, slot_counts)
    moment_new = BETA_ONE * moment_one + (1.0 - BETA_ONE) * projected
    second_new = BETA_TWO * moment_two + (1.0 - BETA_TWO) * projected * projected
    normed = moment_new / (jnp.sqrt(second_new) + EPSILON)
    expanded = jnp.einsum(
        "krq,kqc->krc",
        basis_slot,
        lax.all_gather(normed, "shard", axis=1, tiled=True),
        precision=HIGHEST_PREC,
    )
    update = (GALORE_SCALE * expanded).astype(jnp.bfloat16)
    return (basis_slot, moment_new, second_new, update)


def solution(mesh):
    in_specs = (
        P("owner", "shard", None),
        P("owner", "shard", None),
        P("owner", "shard", None),
        P("owner", "shard", None),
        P(),
        P(),
    )
    out_specs = (
        P("owner", "shard", None),
        P("owner", "shard", None),
        P("owner", "shard", None),
        P("owner", "shard", None),
    )
    return jax.shard_map(
        on_device, mesh=mesh, in_specs=in_specs, out_specs=out_specs, check_vma=False
    )
```

profile of v0, /device:TPU:1, one launch (start us, length us, event | category | flops | bytes accessed | tf_op | source)
XLA Modules:
  0.0 883.1 jit_solution(13709281338159190592)
XLA Ops:
  7.2 0.7 reshape.109
  7.9 0.1 copy.29
  8.0 0.1 convert_reduce_fusion
  8.1 17.2 %fusion.10 = f32[16,256,768]{2,0,1:T(8,128)} fusion(f32[8,256,768]{2,1,0:T(8,128)} %param.8, f32[16,8]{0,1:T(8,128)S(1)} %convert_reduce_fusion), kind=kOutput, calls=%fused_computation.30 | convolution fusion | flops 301989888 | bytes 18874880 | tf_op jit(solution)/shard_map/oi,irc->orc/dot_general | solution.py:55
  25.3 16.4 %copy.31 = f32[16,256,768]{2,1,0:T(8,128)} copy(f32[16,256,768]{2,0,1:T(8,128)} %fusion.10) | data formatting | bytes 25165824 | tf_op jit(solution)/shard_map/oi,irc->orc/dot_general | solution.py:55
  41.7 148.7 %all_to_all.47 = f32[16,256,768]{2,1,0:T(8,128)} all-to-all(f32[16,256,768]{2,1,0:T(8,128)} %copy.31), channel_id=1, replica_groups=mesh['shard'=8,'owner'=16] {'owner'}, dimensions={0} | all-to-all | bytes 25165824 | tf_op jit(solution)/shard_map/all_to_all | solution.py:56
  190.4 6.1 all-to-all-start
  196.5 16.5 %fusion.8 = f32[8,256,768]{2,0,1:T(8,128)S(1)} fusion(f32[16,256,768]{2,1,0:T(8,128)} %all_to_all.47, s32[8]{0:T(128)S(1)} %get-tuple-element.55), kind=kOutput, calls=%fused_computation.28 | convolution fusion | flops 301990016 | bytes 18874400 | tf_op jit(solution)/shard_map/jh,hrc->jrc/dot_general | solution.py:57
  213.1 4.6 copy.33
  217.7 0.0 copy-start.4
  217.7 5.7 all-to-all-done
  223.3 0.0 copy-start
  223.3 1.3 copy-done
  224.7 5.5 all-to-all-start.2
  230.1 0.0 all-gather.2.cloned.1.call-start
  230.2 0.0 copy-done.4
  230.2 0.2 select_reduce_fusion.2
  230.3 0.6 fusion.17
  231.0 1.9 copy.37
  232.9 68.6 %all-to-all-done.2 = f32[8,256,768]{2,1,0:T(8,128)} async-done(((f32[8,256,768]{2,1,0:T(8,128)}), f32[8,256,768]{2,1,0:T(8,128)}, u32[]{:S(2)}, u32[]{:S(2)}) %all-to-all-start.2) | async-done | bytes 6291488 | tf_op jit(solution)/shard_map/all_to_all | solution.py:26
  301.5 0.8 while.13
  302.4 7.6 convolution_bitcast_fusion
  309.9 0.0 copy-start.2
  309.9 0.0 copy-start.3
  309.9 0.8 copy.35
  310.8 491.6 %all_to_all.48 = f32[1,256,768]{2,0,1:T(1,128)S(1)} all-to-all(f32[1,256,768]{2,0,1:T(1,128)S(1)} %copy.35), channel_id=1, replica_groups=mesh['shard'=8,'owner'=16] {'shard'}, dimensions={1} | all-to-all | bytes 1572864 | tf_op jit(solution)/shard_map/all_to_all | solution.py:38
  802.4 0.1 copy.40
  802.4 0.0 copy-done.2
  802.4 0.0 copy-done.3
  802.5 1.6 add_divide_fusion
  804.1 0.0 all-gather.2.cloned.1.call-update
  804.1 3.6 copy.38
  807.7 53.4 %all_to_all.49 = f32[1,2048,256]{2,0,1:T(1,128)S(1)} all-to-all(f32[1,2048,256]{2,0,1:T(1,128)} %copy.38), channel_id=1, replica_groups=mesh['shard'=8,'owner'=16] {'shard'}, dimensions={1} | all-to-all | bytes 4194304 | tf_op jit(solution)/shard_map/all_to_all | solution.py:37
  861.1 0.1 copy.39
  861.2 0.0 copy-start.1
  861.3 3.4 all-gather.2.cloned.1.call-done
  864.7 11.6 %multiply_convert_fusion = bf16[8,256,768]{2,1,0:T(8,128)(2,1)} fusion(f32[8,256,256]{2,1,0:T(8,128)S(1)} %bitcast.92, f32[8,256,768]{2,1,0:T(8,128)} %all-gather.2.cloned.1.call-done), kind=kOutput, calls=%fused_computation.32 | convolution fusion | flops 4834983936 | bytes 11534336 | tf_op jit(solution)/shard_map/krq,kqc->krc/dot_general | solution.py:62
  876.3 0.0 copy-done.1
  (2 shorter events, 0.0 us)
Async XLA Ops:
  190.4 32.9 %all-to-all-start = ((f32[8,256,256]{2,1,0:T(8,128)}), f32[8,256,256]{2,1,0:T(8,128)S(1)}, u32[]{:S(2)}, u32[]{:S(2)}) async-start(f32[8,256,256]{2,1,0:T(8,128)} %param.9), calls=%async_computation | async-start | bytes 4194304 | tf_op jit(solution)/shard_map/all_to_all | solution.py:27
  217.7 12.5 %copy-start.4 = (s32[128]{0:T(128)S(1)}, s32[128]{0:T(128)}, u32[]{:S(2)}) copy-start(s32[128]{0:T(128)} %param.13) | copy-start | bytes 1540
  223.3 1.3 copy-start
  224.7 76.9 %all-to-all-start.2 = ((f32[8,256,768]{2,1,0:T(8,128)}), f32[8,256,768]{2,1,0:T(8,128)}, u32[]{:S(2)}, u32[]{:S(2)}) async-start(f32[8,256,768]{2,1,0:T(8,128)} %copy.33), calls=%async_computation.2 | async-start | bytes 12582912 | tf_op jit(solution)/shard_map/all_to_all | solution.py:26
  230.1 634.5 %all-gather.2.cloned.1.call-start = ((), (), s32[]{:S(2)}) async-start(), calls=%async_computation.5 | async-start | bytes 7077888 | tf_op jit(solution)/shard_map/all_gather | solution.py:65
  309.9 492.5 %copy-start.2 = (f32[8,32,768]{2,1,0:T(8,128)S(1)}, f32[8,32,768]{2,1,0:T(8,128)}, u32[]{:S(2)}) copy-start(f32[8,32,768]{2,1,0:T(8,128)} %param.11) | copy-start | bytes 2359300
  309.9 492.5 %copy-start.3 = (f32[8,32,768]{2,1,0:T(8,128)S(1)}, f32[8,32,768]{2,1,0:T(8,128)}, u32[]{:S(2)}) copy-start(f32[8,32,768]{2,1,0:T(8,128)} %param.10) | copy-start | bytes 2359300
  861.2 15.0 %copy-start.1 = (f32[1,2048,256]{2,1,0:T(8,128)}, f32[1,2048,256]{2,1,0:T(8,128)S(1)}, u32[]{:S(2)}) copy-start(f32[1,2048,256]{2,1,0:T(8,128)S(1)} %copy.39) | copy-start | bytes 6291460
Sparse Core Ops, SparseCore 0:
  804.2 60.3 all-gather.1
where the time goes:
time: 888 us; the launch traced here: 883 us
  blocking collectives  694 us (78%)
  waiting for transfers between devices  77.7 us (9%)
  matrix products  52.9 us (6%)
  local copies, waits for them, and re-layouts  29.7 us (3%)
  between operations  14.1 us (2%)
  starting transfers between devices  11.6 us (1%)
    all_to_all x1, blocking collectives, refresh_project(): lax.all_to_all(projected[None], 'shard', split_axis=1, concat_axis=0, til...  492 us
    all_to_all x1, blocking collectives, on_device(): lax.all_to_all(outgoing, 'owner', split_axis=0, concat_axis=0, tiled=True)  149 us
    all_to_all x1, waiting for transfers between devices, refresh_project(): lax.all_to_all(grad_slices, 'shard', split_axis=0, concat_axis=1, tiled=T...  68.6 us
    all_to_all x1, blocking collectives, refresh_project(): lax.all_to_all(basis_new[None], 'shard', split_axis=1, concat_axis=0, til...  53.4 us
  transfers between devices with their start and end apart: 3, of which 3 were waited for; matrix products, arithmetic and copies ran while one was open for 3% of the time, Pallas kernels for 0%

commit v1 on v0

v1 whole, which is shorter than its diff:
```python
import jax, jax.numpy as jnp
from jax import lax
from jax.experimental import pallas as pl
from jax.sharding import PartitionSpec as P
from jax.experimental.pallas import tpu as pltpu

BF = jnp.bfloat16
F32 = jnp.float32

def split(x):
    hi = x.astype(BF)
    return hi, (x - hi.astype(F32)).astype(BF)

def mm(a, b, dims):
    return lax.dot_general(a, b, (dims, ((), ())), preferred_element_type=F32)

NN = ((1,), (0,))
TN = ((0,), (0,))
NT = ((1,), (1,))

def dot3(a, b, dims):
    ah, al = a
    bh, bl = b
    return mm(ah, bh, dims) + (mm(ah, bl, dims) + mm(al, bh, dims))

NB = 16

def factor(c_ref, rx, rh, rl):
    n = c_ref.shape[0]
    sub = lax.broadcasted_iota(jnp.int32, (NB, 128), 0)
    row = lax.broadcasted_iota(jnp.int32, (NB, n), 0)
    lane = lax.broadcasted_iota(jnp.int32, (NB, n), 1)
    for p in range(n // NB):
        lo = p * NB
        s_a = c_ref[lo:lo + NB, :]
        s_i = jnp.where(lane == row + lo, 1.0, 0.0)
        if p > 0:
            lh, ll = rh[0:lo, 0:n], rl[0:lo, 0:n]
            ch, cl = lh[:, lo:lo + NB], ll[:, lo:lo + NB]
            s_a = s_a - dot3((ch, cl), (lh, ll), TN)
            xh, xl = rh[0:lo, n:2 * n], rl[0:lo, n:2 * n]
            s_i = s_i - dot3((ch, cl), (xh, xl), TN)
        cols = [jnp.broadcast_to(s_a[:, lo + k:lo + k + 1], (NB, 128)) for k in range(NB)]
        pivots = []
        for j in range(NB):
            d = cols[j][j:j + 1, :]
            r = 1.0 / d
            pivots.append(d)
            m = jnp.where(sub > j, cols[j] * r, 0.0)
            for k in range(j + 1, NB):
                cols[k] = cols[k] - m * cols[k][j:j + 1, :]
            m2 = jnp.concatenate([m] * (n // 128), axis=1)
            s_a = s_a - m2 * s_a[j:j + 1, :]
            s_i = s_i - m2 * s_i[j:j + 1, :]
        piv = jnp.concatenate(pivots, axis=0)
        scale = lax.rsqrt(piv)
        scale = jnp.concatenate([scale] * (n // 128), axis=1)
        r_a = jnp.where(lane >= lo + row, s_a * scale, 0.0)
        r_i = s_i * scale
        out = jnp.concatenate([r_a, r_i], axis=1)
        rx[lo:lo + NB, :] = out
        hi = out.astype(BF)
        rh[lo:lo + NB, :] = hi
        rl[lo:lo + NB, :] = (out - hi.astype(F32)).astype(BF)

def body(cnt, g_ref, p_ref, ret_ref, gh, gl, k_h, k_l, z_ref, m_ref, w_ref, c_ref, rx, rh, rl):
    count = cnt[0]
    rows, cols = g_ref.shape
    rank = p_ref.shape[1]
    step = 256
    z_ref[...] = jnp.zeros_like(z_ref)

    @pl.loop(0, rows // step)
    def _(i):
        at = pl.ds(pl.multiple_of(i * step, step), step)
        h, l = split(g_ref[at, :])
        gh[at, :] = h
        gl[at, :] = l
        z_ref[...] += dot3((h, l), split(p_ref[at, :]), TN)

    @pl.when(count > 0)
    def _():
        ct = cols // 256
        for a in range(ct):
            ra = slice(256 * a, 256 * a + 256)
            for b in range(a, ct):
                rb = slice(256 * b, 256 * b + 256)
                blk = mm(gh[:, ra], gh[:, rb], TN) + (mm(gh[:, ra], gl[:, rb], TN) + mm(gl[:, ra], gh[:, rb], TN))
                h, l = split(blk)
                k_h[ra, rb] = h
                k_l[ra, rb] = l
                if b > a:
                    h, l = split(blk.T)
                    k_h[rb, ra] = h
                    k_l[rb, ra] = l

    @pl.loop(0, count)
    def _(it):
        z = split(z_ref[...])
        w_ref[...] = dot3((k_h[...], k_l[...]), z, NN)
        w = split(w_ref[...])
        c_ref[...] = dot3(z, w, TN)
        factor(c_ref, rx, rh, rl)
        x = (rh[:, rank:], rl[:, rank:])
        z_ref[...] = dot3(w, x, NT)

        @pl.when(it == count - 1)
        def _():
            m_ref[...] = dot3(z, x, NT)

    @pl.when(count > 0)
    def _():
        mh, ml = split(m_ref[...])

        @pl.loop(0, rows // step)
        def _(i):
            at = pl.ds(pl.multiple_of(i * step, step), step)
            ret_ref[i, 0:step, :] = dot3((gh[at, :], gl[at, :]), (mh, ml), NN)

    @pl.when(count == 0)
    def _():
        @pl.loop(0, rows // step)
        def _(i):
            at = pl.ds(pl.multiple_of(i * step, step), step)
            ret_ref[i, 0:step, :] = p_ref[at, :]

    for c in range(cols // 256):
        t = z_ref[256 * c:256 * c + 256, :].T
        for s in range(rows // step):
            ret_ref[s, step + 32 * c:step + 32 * c + 32, :] = t[32 * s:32 * s + 32, :]

def refresh(count, g, p):
    rows, cols = g.shape
    rank = p.shape[1]
    V = pltpu.VMEM
    return pl.pallas_call(
        body,
        out_shape=jax.ShapeDtypeStruct((rows // 256, 256 + 96, rank), F32),
        in_specs=[pl.BlockSpec(memory_space=pltpu.SMEM), pl.BlockSpec(memory_space=V), pl.BlockSpec(memory_space=V)],
        out_specs=pl.BlockSpec(memory_space=V),
        scratch_shapes=[V((rows, cols), BF), V((rows, cols), BF), V((cols, cols), BF), V((cols, cols), BF),
                        V((cols, rank), F32), V((cols, rank), F32), V((cols, rank), F32), V((rank, rank), F32),
                        V((rank, 2 * rank), F32), V((rank, 2 * rank), BF), V((rank, 2 * rank), BF)],
        compiler_params=pltpu.CompilerParams(vmem_limit_bytes=56 * 1024 * 1024),
        name="refresh",
    )(count, g, p)


BETA_ONE = 0.9
BETA_TWO = 0.99
EPSILON = 1e-08
GALORE_SCALE = 0.25


def update_body(b_ref, n_ref, o_ref):
    o_ref[0] = (GALORE_SCALE * dot3(split(b_ref[0]), split(n_ref[0]), NN)).astype(BF)


def make_update(basis, normed):
    slots, rows, rank = basis.shape
    cols = normed.shape[2]
    return pl.pallas_call(
        update_body,
        grid=(slots,),
        out_shape=jax.ShapeDtypeStruct((slots, rows, cols), BF),
        in_specs=[
            pl.BlockSpec((1, rows, rank), lambda i: (i, 0, 0)),
            pl.BlockSpec((1, rank, cols), lambda i: (i, 0, 0)),
        ],
        out_specs=pl.BlockSpec((1, rows, cols), lambda i: (i, 0, 0)),
        compiler_params=pltpu.CompilerParams(vmem_limit_bytes=32 * 1024 * 1024),
        name="update",
    )(basis, normed)


def pick(array, index):
    return jnp.stack([lax.dynamic_index_in_dim(array, index[i], 0, keepdims=False) for i in range(index.shape[0])])


def on_device(gradient, old_basis, moment_one, moment_two, slot_expert, cost):
    slots = gradient.shape[0]
    owners = lax.axis_size("owner")
    owner_now = lax.axis_index("owner")
    shard_now = lax.axis_index("shard")
    table = slot_expert.reshape(owners, slots)
    mine = lax.dynamic_index_in_dim(table, owner_now, 0, keepdims=False)
    homes = jnp.arange(owners)
    slot_for = jnp.sum(jnp.where(mine[None, :] // slots == homes[:, None], jnp.arange(slots)[None, :], 0), axis=1)
    own_ids = owner_now * slots + jnp.arange(slots)
    hits = table[None, :, :] == own_ids[:, None, None]
    holder = jnp.sum(jnp.where(hits, homes[None, :, None], 0), axis=(1, 2))
    expert_for = jnp.sum(jnp.where(hits, jnp.arange(slots)[:, None, None], 0), axis=(0, 2))
    count = lax.dynamic_slice_in_dim(cost, owner_now * slots + shard_now, 1)

    grad_whole = lax.all_to_all(gradient, "shard", split_axis=0, concat_axis=1, tiled=True)
    basis_there = lax.all_to_all(pick(old_basis, slot_for), "owner", split_axis=0, concat_axis=0, tiled=True)
    basis_whole = lax.all_to_all(pick(basis_there, holder), "shard", split_axis=0, concat_axis=1, tiled=True)
    result = refresh(count, grad_whole[0], basis_whole[0])
    result = lax.all_to_all(result, "shard", split_axis=0, concat_axis=0, tiled=True)
    result = lax.all_to_all(pick(result, expert_for), "owner", split_axis=0, concat_axis=0, tiled=True)
    result = pick(result, mine // slots)
    basis_slot = result[:, :256, :]
    projected = jnp.concatenate([result[:, 256 + 32 * c : 288 + 32 * c, :] for c in range(3)], axis=2)
    moment_new = BETA_ONE * moment_one + (1.0 - BETA_ONE) * projected
    second_new = BETA_TWO * moment_two + (1.0 - BETA_TWO) * projected * projected
    normed = moment_new / (jnp.sqrt(second_new) + EPSILON)
    update = make_update(basis_slot, lax.all_gather(normed, "shard", axis=1, tiled=True))
    return (basis_slot, moment_new, second_new, update)


def solution(mesh):
    spec = P("owner", "shard", None)
    return jax.shard_map(
        on_device, mesh=mesh, in_specs=(spec,) * 4 + (P(), P()), out_specs=(spec,) * 4, check_vma=False
    )
```

time: 888 us -> 512 us (0.58)
  blocking collectives: 694 us -> 58.5 us
  waiting for transfers between devices: 77.7 us -> 183 us
  between operations: 14.1 us -> 106 us
  starting transfers between devices: 11.6 us -> 83.2 us
  matrix products: 52.9 us -> 0 us
  local copies, waits for them, and re-layouts: 29.7 us -> 60.7 us
  Pallas kernels: 0 us -> 16.1 us
    all_to_all x3 -> x1, blocking collectives: 694 us -> 58.5 us  [on_device(): lax.all_to_all(pick(old_basis, slot_for), 'owner', split_axis=0, concat_a...]
    all_to_all x2 -> x4, starting transfers between devices: 11.6 us -> 83.2 us  [the longest x1 47.1 us: on_device(): lax.all_to_all(pick(result, expert_for), 'owner', split_axis=0, concat_ax...]
    all_to_all x2 -> x4, waiting for transfers between devices: 74.3 us -> 144 us  [the longest x1 69 us: on_device(): lax.all_to_all(pick(result, expert_for), 'owner', split_axis=0, concat_ax...]
    dot_general x4 -> x0, matrix products: 52.9 us -> none  [the longest x1 17.2 us: on_device(): jnp.einsum('oi,irc->orc', send_pick, gradient, precision=HIGHEST_PREC)]
    unnamed x12 -> x62, local copies, waits for them, and re-layouts: 1.53 us -> 51.1 us
    all_gather x1, waiting for transfers between devices: 3.4 us -> 38.8 us  [on_device(): lax.all_gather(normed, 'shard', axis=1, tiled=True)]
    dot_general x2 -> x0, local copies, waits for them, and re-layouts: 21 us -> none  [the longest x1 16.4 us: on_device(): jnp.einsum('oi,irc->orc', send_pick, gradient, precision=HIGHEST_PREC)]
    pallas_call x0 -> x2, Pallas kernels: none -> 16.1 us  [the longest x1 10.6 us: refresh(): pl.pallas_call(body, out_shape=jax.ShapeDtypeStruct((rows // 256, 256 + 9...]
  transfers between devices with their start and end apart: 3 -> 5, of which waited for: 3 -> 5; matrix products, arithmetic and copies ran while one was open for 3% -> 2% of each run, Pallas kernels for 0% -> 0%
where the time goes in v1:
time: 512 us; the launch traced here: 509 us
  waiting for transfers between devices  183 us (36%)
  between operations  106 us (21%)
  starting transfers between devices  83.2 us (16%)
  local copies, waits for them, and re-layouts  60.7 us (12%)
  blocking collectives  58.5 us (11%)
  Pallas kernels  16.1 us (3%)
    all_to_all x1, waiting for transfers between devices, on_device(): lax.all_to_all(pick(result, expert_for), 'owner', split_axis=0, concat_ax...  69 us
    all_to_all x1, blocking collectives, on_device(): lax.all_to_all(pick(old_basis, slot_for), 'owner', split_axis=0, concat_a...  58.5 us
    unnamed x62, local copies, waits for them, and re-layouts  51.1 us
    all_to_all x1, starting transfers between devices, on_device(): lax.all_to_all(pick(result, expert_for), 'owner', split_axis=0, concat_ax...  47.1 us
    all_to_all x1, waiting for transfers between devices, on_device(): lax.all_to_all(gradient, 'shard', split_axis=0, concat_axis=1, tiled=True)  45.9 us
    all_gather x1, waiting for transfers between devices, on_device(): lax.all_gather(normed, 'shard', axis=1, tiled=True)  38.8 us
    all_to_all x1, waiting for transfers between devices, on_device(): lax.all_to_all(pick(basis_there, holder), 'shard', split_axis=0, concat_a...  25.8 us
    all_to_all x1, starting transfers between devices, on_device(): lax.all_to_all(result, 'shard', split_axis=0, concat_axis=0, tiled=True)  25.1 us
  transfers between devices with their start and end apart: 5, of which 5 were waited for; matrix products, arithmetic and copies ran while one was open for 2% of the time, Pallas kernels for 0%

profile of v1, /device:TPU:1, one launch (start us, length us, event | category | flops | bytes accessed | tf_op | source)
XLA Modules:
  0.0 509.4 jit_solution(17778601047502044013)
XLA Ops:
  7.2 0.9 reshape.24
  30.2 1.7 dynamic-slice_dynamic-update-slice_fusion.47
  32.5 1.7 dynamic-slice_dynamic-update-slice_fusion.46
  34.8 1.7 dynamic-slice_dynamic-update-slice_fusion.45
  37.1 1.7 dynamic-slice_dynamic-update-slice_fusion.44
  39.4 1.7 dynamic-slice_dynamic-update-slice_fusion.43
  41.7 1.7 dynamic-slice_dynamic-update-slice_fusion.42
  44.0 1.7 dynamic-slice_dynamic-update-slice_fusion.41
  46.3 1.7 dynamic-slice_dynamic-update-slice_fusion.40
  59.1 58.5 %all_to_all.33 = f32[16,256,256]{2,1,0:T(8,128)} all-to-all(f32[16,256,256]{2,1,0:T(8,128)} %dynamic-slice_dynamic-update-slice_fusion.32), channel_id=1, replica_groups=mesh['shard'=8,'owner'=16] {'owner'}, dimensions={0} | all-to-all | bytes 8388608 | tf_op jit(solution)/shard_map/all_to_all | solution.py:196
  117.6 6.6 %all-to-all-start = ((f32[8,256,768]{2,1,0:T(8,128)}), f32[8,256,768]{2,1,0:T(8,128)}, u32[]{:S(2)}, u32[]{:S(2)}) async-start(f32[8,256,768]{2,1,0:T(8,128)} %param.6), calls=%async_computation | async-start | bytes 12582912 | tf_op jit(solution)/shard_map/all_to_all | solution.py:195
  140.6 1.0 dynamic-slice_dynamic-update-slice_fusion.31
  141.5 1.0 dynamic-slice_dynamic-update-slice_fusion.30
  142.5 1.0 dynamic-slice_dynamic-update-slice_fusion.29
  143.5 1.0 dynamic-slice_dynamic-update-slice_fusion.28
  144.5 1.0 dynamic-slice_dynamic-update-slice_fusion.27
  145.4 1.0 dynamic-slice_dynamic-update-slice_fusion.26
  146.4 1.0 dynamic-slice_dynamic-update-slice_fusion.25
  147.4 1.0 dynamic-slice_dynamic-update-slice_fusion.24
  148.4 1.3 copy-done.5
  149.7 45.9 %all-to-all-done = f32[8,256,768]{2,1,0:T(8,128)} async-done(((f32[8,256,768]{2,1,0:T(8,128)}), f32[8,256,768]{2,1,0:T(8,128)}, u32[]{:S(2)}, u32[]{:S(2)}) %all-to-all-start) | async-done | bytes 6291488 | tf_op jit(solution)/shard_map/all_to_all | solution.py:195
  195.6 4.4 all-to-all-start.2
  200.6 25.8 %all-to-all-done.2 = f32[8,256,256]{2,1,0:T(8,128)S(1)} async-done(((f32[8,256,256]{2,1,0:T(8,128)}), f32[8,256,256]{2,1,0:T(8,128)S(1)}, u32[]{:S(2)}, u32[]{:S(2)}) %all-to-all-start.2) | async-done | bytes 2097184 | tf_op jit(solution)/shard_map/all_to_all | solution.py:197
  226.4 1.3 copy-done.3
  227.7 10.6 %refresh.1 = f32[8,352,256]{2,1,0:T(8,128)} custom-call(s32[1]{0:T(128)} %dynamic_slice.155.cnt, f32[2048,768]{1,0:T(8,128)} %bitcast.g_ref, f32[2048,256]{1,0:T(8,128)} %bitcast.60), custom_call_target="tpu_custom_call" | custom-call | tf_op jit(solution)/shard_map/refresh/pallas_call | solution.py:136
  238.3 25.1 %all-to-all-start.3 = ((f32[8,352,256]{2,1,0:T(8,128)}), f32[8,352,256]{2,1,0:T(8,128)S(1)}, u32[]{:S(2)}, u32[]{:S(2)}) async-start(f32[8,352,256]{2,1,0:T(8,128)} %refresh.1), calls=%async_computation.3 | async-start | bytes 5767168 | tf_op jit(solution)/shard_map/all_to_all | solution.py:199
  294.8 3.3 all-to-all-done.3
  302.7 0.8 dynamic-slice_dynamic-update-slice_fusion.17
  304.3 0.8 dynamic-slice_dynamic-update-slice_fusion.15
  305.1 0.8 dynamic-slice_dynamic-update-slice_fusion.14
  307.4 0.8 dynamic-slice_dynamic-update-slice_fusion.11
  308.2 0.8 dynamic-slice_dynamic-update-slice_fusion.10
  310.5 47.1 %all-to-all-start.4 = ((f32[16,352,256]{2,1,0:T(8,128)}), f32[16,352,256]{2,1,0:T(8,128)}, u32[]{:S(2)}, u32[]{:S(2)}) async-start(f32[16,352,256]{2,1,0:T(8,128)} %dynamic-slice_dynamic-update-slice_fusion.8), calls=%async_computation.4 | async-start | bytes 11534336 | tf_op jit(solution)/shard_map/all_to_all | solution.py:200
  373.3 69.0 %all-to-all-done.4 = f32[16,352,256]{2,1,0:T(8,128)} async-done(((f32[16,352,256]{2,1,0:T(8,128)}), f32[16,352,256]{2,1,0:T(8,128)}, u32[]{:S(2)}, u32[]{:S(2)}) %all-to-all-start.4) | async-done | bytes 5767200 | tf_op jit(solution)/shard_map/all_to_all | solution.py:200
  442.2 1.0 dynamic-slice_dynamic-update-slice_fusion.7
  443.3 1.0 dynamic-slice_dynamic-update-slice_fusion.6
  444.3 1.0 dynamic-slice_dynamic-update-slice_fusion.5
  445.3 1.0 dynamic-slice_dynamic-update-slice_fusion.4
  446.3 1.0 dynamic-slice_dynamic-update-slice_fusion.3
  447.3 1.0 dynamic-slice_dynamic-update-slice_fusion.2
  448.4 1.0 dynamic-slice_dynamic-update-slice_fusion.1
  449.4 1.0 dynamic-slice_dynamic-update-slice_fusion
  450.4 1.6 copy-done.4
  452.0 1.7 add_divide_fusion
  453.8 1.8 slice.208.b_ref
  455.6 38.8 %all-gather.2.cloned.1.call-done.n_ref = f32[8,256,768]{2,1,0:T(8,128)} async-done(((f32[8,32,768]{2,1,0:T(8,128)}), f32[8,256,768]{2,1,0:T(8,128)}) %all-gather.2.cloned.1.call-update) | async-done | bytes 6291472 | tf_op jit(solution)/shard_map/all_gather | solution.py:207
  494.4 2.8 copy-done.1
  497.1 5.4 %update.1 = bf16[8,256,768]{2,1,0:T(8,128)(2,1)} custom-call(f32[8,256,256]{2,1,0:T(8,128)S(1)} %slice.208.b_ref, f32[8,256,768]{2,1,0:T(8,128)S(1)} %copy-done.1), custom_call_target="tpu_custom_call" | custom-call | tf_op jit(solution)/shard_map/update/pallas_call | solution.py:162
  (47 shorter events, 18.2 us)
Async XLA Ops:
  7.2 41.5 %copy-start.2 = (f32[8,256,256]{2,1,0:T(8,128)S(1)}, f32[8,256,256]{2,1,0:T(8,128)}, u32[]{:S(2)}) copy-start(f32[8,256,256]{2,1,0:T(8,128)} %param.7) | copy-start | bytes 6291460
  117.6 78.0 %all-to-all-start = ((f32[8,256,768]{2,1,0:T(8,128)}), f32[8,256,768]{2,1,0:T(8,128)}, u32[]{:S(2)}, u32[]{:S(2)}) async-start(f32[8,256,768]{2,1,0:T(8,128)} %param.6), calls=%async_computation | async-start | bytes 12582912 | tf_op jit(solution)/shard_map/all_to_all | solution.py:195
  140.5 59.5 %copy-start.8 = (s32[128]{0:T(128)S(1)}, s32[128]{0:T(128)}, u32[]{:S(2)}) copy-start(s32[128]{0:T(128)} %param.11) | copy-start | bytes 1540
  148.4 1.3 copy-start.5
  195.6 30.7 %all-to-all-start.2 = ((f32[8,256,256]{2,1,0:T(8,128)}), f32[8,256,256]{2,1,0:T(8,128)S(1)}, u32[]{:S(2)}, u32[]{:S(2)}) async-start(f32[8,256,256]{2,1,0:T(8,128)} %copy-done.5), calls=%async_computation.2 | async-start | bytes 4194304 | tf_op jit(solution)/shard_map/all_to_all | solution.py:197
  226.4 1.3 copy-start.3
  238.3 59.9 %all-to-all-start.3 = ((f32[8,352,256]{2,1,0:T(8,128)}), f32[8,352,256]{2,1,0:T(8,128)S(1)}, u32[]{:S(2)}, u32[]{:S(2)}) async-start(f32[8,352,256]{2,1,0:T(8,128)} %refresh.1), calls=%async_computation.3 | async-start | bytes 5767168 | tf_op jit(solution)/shard_map/all_to_all | solution.py:199
  310.5 131.7 %all-to-all-start.4 = ((f32[16,352,256]{2,1,0:T(8,128)}), f32[16,352,256]{2,1,0:T(8,128)}, u32[]{:S(2)}, u32[]{:S(2)}) async-start(f32[16,352,256]{2,1,0:T(8,128)} %dynamic-slice_dynamic-update-slice_fusion.8), calls=%async_computation.4 | async-start | bytes 11534336 | tf_op jit(solution)/shard_map/all_to_all | solution.py:200
  357.6 94.4 %copy-start.6 = (f32[8,32,768]{2,1,0:T(8,128)S(1)}, f32[8,32,768]{2,1,0:T(8,128)}, u32[]{:S(2)}) copy-start(f32[8,32,768]{2,1,0:T(8,128)} %param.9) | copy-start | bytes 2359300
  357.7 94.4 %copy-start.7 = (f32[8,32,768]{2,1,0:T(8,128)S(1)}, f32[8,32,768]{2,1,0:T(8,128)}, u32[]{:S(2)}) copy-start(f32[8,32,768]{2,1,0:T(8,128)} %param.8) | copy-start | bytes 2359300
  357.7 136.7 %all-gather.2.cloned.1.call-start = ((), (), s32[]{:S(2)}) async-start(), calls=%async_computation.5 | async-start | bytes 7077888 | tf_op jit(solution)/shard_map/all_gather | solution.py:207
  450.4 1.6 copy-start.4
  455.6 47.0 %copy-start = (f32[8,256,256]{2,1,0:T(8,128)}, f32[8,256,256]{2,1,0:T(8,128)S(1)}, u32[]{:S(2)}) copy-start(f32[8,256,256]{2,1,0:T(8,128)S(1)} %slice.208.b_ref) | copy-start | bytes 6291460
  494.4 2.8 copy-start.1
Sparse Core Ops, SparseCore 0:
  453.9 40.4 all-gather.1

commit v2 on v1

--- a/solution.py
+++ b/solution.py
@@ -1,3 +1,4 @@
+import functools
 import jax, jax.numpy as jnp
 from jax import lax
 from jax.experimental import pallas as pl
@@ -63,41 +64,187 @@
         rh[lo:lo + NB, :] = hi
         rl[lo:lo + NB, :] = (out - hi.astype(F32)).astype(BF)
 
-def body(cnt, g_ref, p_ref, ret_ref, gh, gl, k_h, k_l, z_ref, m_ref, w_ref, c_ref, rx, rh, rl):
+MESH = pl.DeviceIdType.MESH
+V = pltpu.VMEM
+
+
+def greet(groups):
+    barrier = pltpu.get_barrier_semaphore()
+    total = 0
+    for axis, size in groups:
+        me = lax.axis_index(axis)
+
+        @pl.loop(1, size)
+        def _(d):
+            pl.semaphore_signal(barrier, inc=1, device_id={axis: lax.rem(me + d, size)}, device_id_type=MESH)
+
+        total += size - 1
+    pl.semaphore_wait(barrier, total)
+
+
+def remote(src, dst, send, recv, axis, target):
+    return pltpu.make_async_remote_copy(
+        src_ref=src, dst_ref=dst, send_sem=send, recv_sem=recv, device_id={axis: target}, device_id_type=MESH
+    )
+
+
+def enter_body(shards, owners, slot_ref, holder_ref, g_ref, b_ref, gh_out, gl_out, kh_out, kl_out, z_out, p_out,
+               gland, gh, gl, kacc, stage, landed, stage2, pland,
+               g_send, g_recv, a_send, a_recv, b_send, b_recv, own_sem, h_sem, l_sem):
+    s_me = lax.axis_index("shard")
+    o_me = lax.axis_index("owner")
+    greet((("shard", shards), ("owner", owners)))
+
+    def at_shard(d):
+        return lax.rem(s_me + d, shards)
+
+    def from_shard(d):
+        return lax.rem(s_me - d + shards, shards)
+
+    def at_owner(d):
+        return lax.rem(o_me + d, owners)
+
+    def from_owner(d):
+        return lax.rem(o_me - d + owners, owners)
+
+    own = pltpu.make_async_copy(g_ref.at[s_me], gland.at[s_me], own_sem)
+    own.start()
+
+    @pl.loop(1, owners)
+    def _(d):
+        t = at_owner(d)
+        stage[t] = b_ref[slot_ref[t]]
+        remote(stage.at[t], landed.at[o_me], a_send.at[d], a_recv.at[d], "owner", t).start()
+
+    @pl.loop(1, shards)
+    def _(d):
+        t = at_shard(d)
+        remote(g_ref.at[t], gland.at[s_me], g_send.at[d], g_recv.at[d], "shard", t).start()
+
+    landed[o_me] = b_ref[slot_ref[o_me]]
+    kacc[...] = jnp.zeros_like(kacc)
+    own.wait()
+    tiles = kacc.shape[0] // 256
+
+    def gram(f):
+        h, l = split(gland[f])
+        gh[f] = h
+        gl[f] = l
+        pltpu.make_async_copy(gh.at[f], gh_out.at[f], h_sem.at[f]).start()
+        pltpu.make_async_copy(gl.at[f], gl_out.at[f], l_sem.at[f]).start()
+        for a in range(tiles):
+            ra = slice(256 * a, 256 * a + 256)
+            for b in range(a, tiles):
+                rb = slice(256 * b, 256 * b + 256)
+                kacc[ra, rb] += dot3((h[:, ra], l[:, ra]), (h[:, rb], l[:, rb]), TN)
+
+    gram(s_me)
+
+    def take_gram(d):
+        f = from_shard(d)
+        remote(g_ref.at[at_shard(d)], gland.at[f], g_send.at[d], g_recv.at[d], "shard", at_shard(d)).wait_recv()
+        gram(f)
+
+    half = EARLY
+    pl.loop(1, half)(take_gram)
+
+    @pl.loop(1, owners)
+    def _(d):
+        remote(stage.at[at_owner(d)], landed.at[from_owner(d)], a_send.at[d], a_recv.at[d], "owner", at_owner(d)).wait()
+
+    @pl.loop(1, shards)
+    def _(d):
+        t = at_shard(d)
+        stage2[t] = landed[holder_ref[t]]
+        remote(stage2.at[t], pland.at[s_me], b_send.at[d], b_recv.at[d], "shard", t).start()
+
+    pland[s_me] = landed[holder_ref[s_me]]
+    pl.loop(half, shards)(take_gram)
+
+    for a in range(tiles):
+        ra = slice(256 * a, 256 * a + 256)
+        for b in range(a, tiles):
+            rb = slice(256 * b, 256 * b + 256)
+            h, l = split(kacc[ra, rb])
+            kh_out[ra, rb] = h
+            kl_out[ra, rb] = l
+            if b > a:
+                h, l = split(kacc[ra, rb].T)
+                kh_out[rb, ra] = h
+                kl_out[rb, ra] = l
+
+    def project(f):
+        p_out[f] = pland[f]
+        return dot3((gh[f], gl[f]), split(pland[f]), TN)
+
+    z_out[...] = project(s_me)
+
+    @pl.loop(1, shards)
+    def _(d):
+        f = from_shard(d)
+        remote(stage2.at[at_shard(d)], pland.at[f], b_send.at[d], b_recv.at[d], "shard", at_shard(d)).wait()
+        z_out[...] += project(f)
+
+    @pl.loop(1, shards)
+    def _(d):
+        remote(g_ref.at[at_shard(d)], gland.at[from_shard(d)], g_send.at[d], g_recv.at[d], "shard", at_shard(d)).wait_send()
+
+    @pl.loop(0, shards)
+    def _(f):
+        pltpu.make_async_copy(gh.at[f], gh_out.at[f], h_sem.at[f]).wait()
+        pltpu.make_async_copy(gl.at[f], gl_out.at[f], l_sem.at[f]).wait()
+
+
+EARLY = 5
+
+
+def enter(slot_for, holder, gradient, basis):
+    shards, rows, cols = gradient.shape
+    rank = basis.shape[2]
+    owners = slot_for.shape[0]
+    sem = pltpu.SemaphoreType.DMA
+    smem = pl.BlockSpec(memory_space=pltpu.SMEM)
+    vmem = pl.BlockSpec(memory_space=V)
+    hbm = pl.BlockSpec(memory_space=pl.ANY)
+    return pl.pallas_call(
+        functools.partial(enter_body, shards, owners),
+        out_shape=(
+            jax.ShapeDtypeStruct((shards, rows, cols), BF),
+            jax.ShapeDtypeStruct((shards, rows, cols), BF),
+            jax.ShapeDtypeStruct((cols, cols), BF),
+            jax.ShapeDtypeStruct((cols, cols), BF),
+            jax.ShapeDtypeStruct((cols, rank), F32),
+            jax.ShapeDtypeStruct((shards, rows, rank), F32),
+        ),
+        in_specs=[smem, smem, hbm, vmem],
+        out_specs=(hbm, hbm, vmem, vmem, vmem, vmem),
+        scratch_shapes=[
+            V((shards, rows, cols), F32), V((shards, rows, cols), BF), V((shards, rows, cols), BF), V((cols, cols), F32),
+            V((owners, rows, rank), F32), V((owners, rows, rank), F32), V((shards, rows, rank), F32), V((shards, rows, rank), F32),
+            sem((shards,)), sem((shards,)), sem((owners,)), sem((owners,)), sem((shards,)), sem((shards,)),
+            sem, sem((shards,)), sem((shards,)),
+        ],
+        compiler_params=pltpu.CompilerParams(
+            collective_id=0, has_side_effects=True, vmem_limit_bytes=56 * 1024 * 1024
+        ),
+        name="enter",
+    )(slot_for, holder, gradient, basis)
+
+
+def body(cnt, gh_hbm, gl_hbm, kh_ref, kl_ref, zin_ref, p_ref, pn_ref, pj_ref, gh, gl, z_ref, m_ref, w_ref, c_ref, rx, rh, rl, sems):
     count = cnt[0]
-    rows, cols = g_ref.shape
-    rank = p_ref.shape[1]
-    step = 256
-    z_ref[...] = jnp.zeros_like(z_ref)
-
-    @pl.loop(0, rows // step)
-    def _(i):
-        at = pl.ds(pl.multiple_of(i * step, step), step)
-        h, l = split(g_ref[at, :])
-        gh[at, :] = h
-        gl[at, :] = l
-        z_ref[...] += dot3((h, l), split(p_ref[at, :]), TN)
-
-    @pl.when(count > 0)
-    def _():
-        ct = cols // 256
-        for a in range(ct):
-            ra = slice(256 * a, 256 * a + 256)
-            for b in range(a, ct):
-                rb = slice(256 * b, 256 * b + 256)
-                blk = mm(gh[:, ra], gh[:, rb], TN) + (mm(gh[:, ra], gl[:, rb], TN) + mm(gl[:, ra], gh[:, rb], TN))
-                h, l = split(blk)
-                k_h[ra, rb] = h
-                k_l[ra, rb] = l
-                if b > a:
-                    h, l = split(blk.T)
-                    k_h[rb, ra] = h
-                    k_l[rb, ra] = l
+    shards, rows, cols = gh.shape
+    rank = p_ref.shape[2]
+    load_h = pltpu.make_async_copy(gh_hbm, gh, sems.at[0])
+    load_l = pltpu.make_async_copy(gl_hbm, gl, sems.at[1])
+    load_h.start()
+    load_l.start()
+    z_ref[...] = zin_ref[...]
 
     @pl.loop(0, count)
     def _(it):
         z = split(z_ref[...])
-        w_ref[...] = dot3((k_h[...], k_l[...]), z, NN)
+        w_ref[...] = dot3((kh_ref[...], kl_ref[...]), z, NN)
         w = split(w_ref[...])
         c_ref[...] = dot3(z, w, TN)
         factor(c_ref, rx, rh, rl)
@@ -108,43 +255,50 @@
         def _():
             m_ref[...] = dot3(z, x, NT)
 
+    for c in range(cols // 256):
+        t = z_ref[256 * c:256 * c + 256, :].T
+        for s in range(shards):
+            part = rank // shards
+            pj_ref[s, :, 256 * c:256 * c + 256] = t[part * s:part * s + part, :]
+
+    load_h.wait()
+    load_l.wait()
+
     @pl.when(count > 0)
     def _():
         mh, ml = split(m_ref[...])
 
-        @pl.loop(0, rows // step)
+        @pl.loop(0, shards)
         def _(i):
-            at = pl.ds(pl.multiple_of(i * step, step), step)
-            ret_ref[i, 0:step, :] = dot3((gh[at, :], gl[at, :]), (mh, ml), NN)
+            pn_ref[i] = dot3((gh[i], gl[i]), (mh, ml), NN)
 
     @pl.when(count == 0)
     def _():
-        @pl.loop(0, rows // step)
-        def _(i):
-            at = pl.ds(pl.multiple_of(i * step, step), step)
-            ret_ref[i, 0:step, :] = p_ref[at, :]
-
-    for c in range(cols // 256):
-        t = z_ref[256 * c:256 * c + 256, :].T
-        for s in range(rows // step):
-            ret_ref[s, step + 32 * c:step + 32 * c + 32, :] = t[32 * s:32 * s + 32, :]
-
-def refresh(count, g, p):
-    rows, cols = g.shape
-    rank = p.shape[1]
-    V = pltpu.VMEM
+        pn_ref[...] = p_ref[...]
+
+
+def refresh(count, gh, gl, kh, kl, z, p):
+    shards, rows, cols = gh.shape
+    rank = p.shape[2]
+    smem = pl.BlockSpec(memory_space=pltpu.SMEM)
+    vmem = pl.BlockSpec(memory_space=V)
+    hbm = pl.BlockSpec(memory_space=pl.ANY)
     return pl.pallas_call(
         body,
-        out_shape=jax.ShapeDtypeStruct((rows // 256, 256 + 96, rank), F32),
-        in_specs=[pl.BlockSpec(memory_space=pltpu.SMEM), pl.BlockSpec(memory_space=V), pl.BlockSpec(memory_space=V)],
-        out_specs=pl.BlockSpec(memory_space=V),
-        scratch_shapes=[V((rows, cols), BF), V((rows, cols), BF), V((cols, cols), BF), V((cols, cols), BF),
-                        V((cols, rank), F32), V((cols, rank), F32), V((cols, rank), F32), V((rank, rank), F32),
-                        V((rank, 2 * rank), F32), V((rank, 2 * rank), BF), V((rank, 2 * rank), BF)],
+        out_shape=(
+            jax.ShapeDtypeStruct((shards, rows, rank), F32),
+            jax.ShapeDtypeStruct((shards, rank // shards, cols), F32),
+        ),
+        in_specs=[smem, hbm, hbm, vmem, vmem, vmem, vmem],
+        out_specs=(vmem, vmem),
+        scratch_shapes=[
+            V((shards, rows, cols), BF), V((shards, rows, cols), BF),
+            V((cols, rank), F32), V((cols, rank), F32), V((cols, rank), F32), V((rank, rank), F32),
+            V((rank, 2 * rank), F32), V((rank, 2 * rank), BF), V((rank, 2 * rank), BF), pltpu.SemaphoreType.DMA((2,)),
+        ],
         compiler_params=pltpu.CompilerParams(vmem_limit_bytes=56 * 1024 * 1024),
         name="refresh",
-    )(count, g, p)
-
+    )(count, gh, gl, kh, kl, z, p)
 
 BETA_ONE = 0.9
 BETA_TWO = 0.99
@@ -192,10 +346,9 @@
     expert_for = jnp.sum(jnp.where(hits, jnp.arange(slots)[:, None, None], 0), axis=(0, 2))
     count = lax.dynamic_slice_in_dim(cost, owner_now * slots + shard_now, 1)
 
-    grad_whole = lax.all_to_all(gradient, "shard", split_axis=0, concat_axis=1, tiled=True)
-    basis_there = lax.all_to_all(pick(old_basis, slot_for), "owner", split_axis=0, concat_axis=0, tiled=True)
-    basis_whole = lax.all_to_all(pick(basis_there, holder), "shard", split_axis=0, concat_axis=1, tiled=True)
-    result = refresh(count, grad_whole[0], basis_whole[0])
+    gh, gl, kh, kl, z, whole = enter(slot_for, holder, gradient, old_basis)
+    basis, projected = refresh(count, gh, gl, kh, kl, z, whole)
+    result = jnp.concatenate([basis] + [projected[:, :, 256 * c : 256 * c + 256] for c in range(3)], axis=1)
     result = lax.all_to_all(result, "shard", split_axis=0, concat_axis=0, tiled=True)
     result = lax.all_to_all(pick(result, expert_for), "owner", split_axis=0, concat_axis=0, tiled=True)
     result = pick(result, mine // slots)

time: 512 us -> 398 us (0.78)
  Pallas kernels: 16.1 us -> 122 us
  waiting for transfers between devices: 183 us -> 111 us
  blocking collectives: 58.5 us -> 0 us
  between operations: 106 us -> 59.8 us
  local copies, waits for them, and re-layouts: 60.7 us -> 31.5 us
  starting transfers between devices: 83.2 us -> 65.8 us
    pallas_call x1 -> x2, Pallas kernels: 10.6 us -> 116 us  [the longest x1 109 us: enter(): pl.pallas_call(functools.partial(enter_body, shards, owners), out_shape=(...]
    all_to_all x2 -> x0, waiting for transfers between devices: 71.7 us -> none  [the longest x1 45.9 us: on_device(): lax.all_to_all(gradient, 'shard', split_axis=0, concat_axis=1, tiled=True)]
    all_to_all x1 -> x0, blocking collectives: 58.5 us -> none  [on_device(): lax.all_to_all(pick(old_basis, slot_for), 'owner', split_axis=0, concat_a...]
    unnamed x62 -> x32, local copies, waits for them, and re-layouts: 51.1 us -> 23.2 us
    all_to_all x1, starting transfers between devices: 25.1 us -> 13.6 us  [on_device(): lax.all_to_all(result, 'shard', split_axis=0, concat_axis=0, tiled=True)]
    all_to_all x2 -> x0, starting transfers between devices: 11 us -> none  [the longest x1 6.61 us: on_device(): lax.all_to_all(gradient, 'shard', split_axis=0, concat_axis=1, tiled=True)]
  transfers between devices with their start and end apart: 5 -> 3, of which waited for: 5 -> 3; matrix products, arithmetic and copies ran while one was open for 2% -> 1% of each run, Pallas kernels for 0% -> 0%
where the time goes in v2:
time: 398 us; the launch traced here: 396 us
  Pallas kernels  122 us (31%)
  waiting for transfers between devices  111 us (28%)
  starting transfers between devices  65.8 us (17%)
  between operations  59.8 us (15%)
  local copies, waits for them, and re-layouts  31.5 us (8%)
  other arithmetic  6.47 us (2%)
    pallas_call x1, Pallas kernels, enter(): pl.pallas_call(functools.partial(enter_body, shards, owners), out_shape=(...  109 us
    all_to_all x1, waiting for transfers between devices, on_device(): lax.all_to_all(pick(result, expert_for), 'owner', split_axis=0, concat_ax...  68.3 us
    all_to_all x1, starting transfers between devices, on_device(): lax.all_to_all(pick(result, expert_for), 'owner', split_axis=0, concat_ax...  52.1 us
    all_gather x1, waiting for transfers between devices, on_device(): lax.all_gather(normed, 'shard', axis=1, tiled=True)  38.6 us
    unnamed x32, local copies, waits for them, and re-layouts  23.2 us
    all_to_all x1, starting transfers between devices, on_device(): lax.all_to_all(result, 'shard', split_axis=0, concat_axis=0, tiled=True)  13.6 us
  transfers between devices with their start and end apart: 3, of which 3 were waited for; matrix products, arithmetic and copies ran while one was open for 1% of the time, Pallas kernels for 0%

profile of v2, /device:TPU:1, one launch (start us, length us, event | category | flops | bytes accessed | tf_op | source)
XLA Modules:
  0.0 396.4 jit_solution(1626668614756498126)
XLA Ops:
  7.2 0.7 reshape.16
  7.9 0.1 copy.10
  8.0 0.6 select_reduce_fusion.slot_ref
  8.6 1.2 dynamic_slice.81.cnt
  9.9 0.8 fusion.2
  10.7 108.6 %enter.1 = (bf16[8,256,768]{2,1,0:T(8,128)(2,1)}, bf16[8,256,768]{2,1,0:T(8,128)(2,1)}, bf16[768,768]{1,0:T(8,128)(2,1)}, bf16[768,768]{1,0:T(8,128)(2,1)}, f32[768,256]{1,0:T(8,128)}, /*index=5*/f32[8,256,256]{2,1,0:T(8,128)}) custom-call(s32[16]{0:T(128)} %select_reduce_fusion.slot_ref, s32[8]{0:T(128)} %get-tuple-element.21.holder_ref, ...), custom_call_target="tpu_custom_call" | custom-call | tf_op jit(solution)/shard_map/enter/pallas_call | solution.py:209
  119.2 7.8 %refresh.1 = (f32[8,256,256]{2,1,0:T(8,128)}, f32[8,32,768]{2,1,0:T(8,128)}) custom-call(s32[1]{0:T(128)} %dynamic_slice.81.cnt, bf16[8,256,768]{2,1,0:T(8,128)(2,1)} %get-tuple-element.12.gh_hbm, bf16[8,256,768]{2,1,0:T(8,128)(2,1)} %get-tuple-element.13.gl_hbm, bf16[768,768]{1,0:T(8,128)(2,1)} %get-tuple-element.14.kh_ref, ...), custom_call_target="tpu_custom_call" | custom-call | tf_op jit(solution)/shard_map/refresh/pallas_call | solution.py:286
  127.0 1.2 fusion.6
  128.2 3.4 pad_maximum_fusion
  131.6 13.6 %all-to-all-start = ((f32[8,352,256]{2,1,0:T(8,128)}), f32[8,352,256]{2,1,0:T(8,128)S(1)}, u32[]{:S(2)}, u32[]{:S(2)}) async-start(f32[8,352,256]{2,1,0:T(8,128)} %pad_maximum_fusion), calls=%async_computation | async-start | bytes 5767168 | tf_op jit(solution)/shard_map/all_to_all | solution.py:352
  145.2 0.7 fusion.8
  175.9 4.0 %all-to-all-done = f32[8,352,256]{2,1,0:T(8,128)S(1)} async-done(((f32[8,352,256]{2,1,0:T(8,128)}), f32[8,352,256]{2,1,0:T(8,128)S(1)}, u32[]{:S(2)}, u32[]{:S(2)}) %all-to-all-start) | async-done | bytes 2883616 | tf_op jit(solution)/shard_map/all_to_all | solution.py:352
  179.9 0.8 dynamic-slice_dynamic-update-slice_fusion.23
  180.7 0.8 dynamic-slice_dynamic-update-slice_fusion.22
  181.5 0.8 dynamic-slice_dynamic-update-slice_fusion.21
  182.2 0.8 dynamic-slice_dynamic-update-slice_fusion.20
  183.0 0.8 dynamic-slice_dynamic-update-slice_fusion.19
  183.8 0.8 dynamic-slice_dynamic-update-slice_fusion.18
  184.5 0.8 dynamic-slice_dynamic-update-slice_fusion.17
  185.3 0.8 dynamic-slice_dynamic-update-slice_fusion.16
  186.1 0.8 dynamic-slice_dynamic-update-slice_fusion.15
  186.9 0.8 dynamic-slice_dynamic-update-slice_fusion.14
  187.7 0.8 dynamic-slice_dynamic-update-slice_fusion.13
  188.5 0.8 dynamic-slice_dynamic-update-slice_fusion.12
  189.3 0.8 dynamic-slice_dynamic-update-slice_fusion.11
  190.0 0.8 dynamic-slice_dynamic-update-slice_fusion.10
  190.8 0.8 dynamic-slice_dynamic-update-slice_fusion.9
  191.6 0.7 dynamic-slice_dynamic-update-slice_fusion.8
  192.3 52.1 %all-to-all-start.1 = ((f32[16,352,256]{2,1,0:T(8,128)}), f32[16,352,256]{2,1,0:T(8,128)}, u32[]{:S(2)}, u32[]{:S(2)}) async-start(f32[16,352,256]{2,1,0:T(8,128)} %dynamic-slice_dynamic-update-slice_fusion.8), calls=%async_computation.1 | async-start | bytes 11534336 | tf_op jit(solution)/shard_map/all_to_all | solution.py:353
  244.5 0.0 all-gather.2.cloned.1.call-start
  244.6 0.7 fusion.7
  260.9 68.3 %all-to-all-done.1 = f32[16,352,256]{2,1,0:T(8,128)} async-done(((f32[16,352,256]{2,1,0:T(8,128)}), f32[16,352,256]{2,1,0:T(8,128)}, u32[]{:S(2)}, u32[]{:S(2)}) %all-to-all-start.1) | async-done | bytes 5767200 | tf_op jit(solution)/shard_map/all_to_all | solution.py:353
  329.2 1.0 dynamic-slice_dynamic-update-slice_fusion.7
  330.3 1.1 dynamic-slice_dynamic-update-slice_fusion.6
  331.4 1.0 dynamic-slice_dynamic-update-slice_fusion.5
  332.4 1.0 dynamic-slice_dynamic-update-slice_fusion.4
  333.4 1.0 dynamic-slice_dynamic-update-slice_fusion.3
  334.5 1.0 dynamic-slice_dynamic-update-slice_fusion.2
  335.5 1.0 dynamic-slice_dynamic-update-slice_fusion.1
  336.5 1.0 dynamic-slice_dynamic-update-slice_fusion
  337.5 1.6 copy-done.2
  339.1 0.1 fusion.5
  339.2 1.7 add_divide_fusion
  340.8 0.0 all-gather.2.cloned.1.call-update
  340.9 1.8 slice.124.b_ref
  342.7 38.6 %all-gather.2.cloned.1.call-done.n_ref = f32[8,256,768]{2,1,0:T(8,128)} async-done(((f32[8,32,768]{2,1,0:T(8,128)}), f32[8,256,768]{2,1,0:T(8,128)}) %all-gather.2.cloned.1.call-update) | async-done | bytes 6291472 | tf_op jit(solution)/shard_map/all_gather | solution.py:360
  381.3 2.8 copy-done.1
  384.1 5.4 %update.1 = bf16[8,256,768]{2,1,0:T(8,128)(2,1)} custom-call(f32[8,256,256]{2,1,0:T(8,128)S(1)} %slice.124.b_ref, f32[8,256,768]{2,1,0:T(8,128)S(1)} %copy-done.1), custom_call_target="tpu_custom_call" | custom-call | tf_op jit(solution)/shard_map/update/pallas_call | solution.py:316
  (11 shorter events, 0.1 us)
Async XLA Ops:
  131.6 48.4 %all-to-all-start = ((f32[8,352,256]{2,1,0:T(8,128)}), f32[8,352,256]{2,1,0:T(8,128)S(1)}, u32[]{:S(2)}, u32[]{:S(2)}) async-start(f32[8,352,256]{2,1,0:T(8,128)} %pad_maximum_fusion), calls=%async_computation | async-start | bytes 5767168 | tf_op jit(solution)/shard_map/all_to_all | solution.py:352
  192.3 136.9 %all-to-all-start.1 = ((f32[16,352,256]{2,1,0:T(8,128)}), f32[16,352,256]{2,1,0:T(8,128)}, u32[]{:S(2)}, u32[]{:S(2)}) async-start(f32[16,352,256]{2,1,0:T(8,128)} %dynamic-slice_dynamic-update-slice_fusion.8), calls=%async_computation.1 | async-start | bytes 11534336 | tf_op jit(solution)/shard_map/all_to_all | solution.py:353
  244.5 136.8 %all-gather.2.cloned.1.call-start = ((), (), s32[]{:S(2)}) async-start(), calls=%async_computation.2 | async-start | bytes 7077888 | tf_op jit(solution)/shard_map/all_gather | solution.py:360
  330.2 8.9 %copy-start.3 = (f32[8,32,768]{2,1,0:T(8,128)S(1)}, f32[8,32,768]{2,1,0:T(8,128)}, u32[]{:S(2)}) copy-start(f32[8,32,768]{2,1,0:T(8,128)} %param.9) | copy-start | bytes 2359300
  330.3 8.9 %copy-start.4 = (f32[8,32,768]{2,1,0:T(8,128)S(1)}, f32[8,32,768]{2,1,0:T(8,128)}, u32[]{:S(2)}) copy-start(f32[8,32,768]{2,1,0:T(8,128)} %param.8) | copy-start | bytes 2359300
  337.5 1.6 copy-start.2
  342.7 46.9 %copy-start = (f32[8,256,256]{2,1,0:T(8,128)}, f32[8,256,256]{2,1,0:T(8,128)S(1)}, u32[]{:S(2)}) copy-start(f32[8,256,256]{2,1,0:T(8,128)S(1)} %slice.124.b_ref) | copy-start | bytes 6291460
  381.3 2.8 copy-start.1
Sparse Core Ops, SparseCore 0:
  341.0 40.2 all-gather.1

commit v3 on v2

--- a/solution.py
+++ b/solution.py
@@ -300,35 +300,176 @@
         name="refresh",
     )(count, gh, gl, kh, kl, z, p)
 
+
 BETA_ONE = 0.9
 BETA_TWO = 0.99
 EPSILON = 1e-08
 GALORE_SCALE = 0.25
-
-
-def update_body(b_ref, n_ref, o_ref):
-    o_ref[0] = (GALORE_SCALE * dot3(split(b_ref[0]), split(n_ref[0]), NN)).astype(BF)
-
-
-def make_update(basis, normed):
-    slots, rows, rank = basis.shape
-    cols = normed.shape[2]
+CHUNKS = 2
+
+
+def leave_body(shards, owners, expert_ref, home_ref, pn_ref, pj_ref, one_ref, two_ref,
+               basis_out, one_out, two_out, update_out,
+               pj1, pj_stage, pj2, pn1a, pn1b, pn_stage, pn2a, pn2b, normed, nh, nl,
+               j_send, j_recv, jo_send, jo_recv, p_send, p_recv, po_send, po_recv, n_send, n_recv, f_send, f_recv, own_sem):
+    s_me = lax.axis_index("shard")
+    o_me = lax.axis_index("owner")
+    pn1, pn2 = (pn1a, pn1b), (pn2a, pn2b)
+    chunk = pn1a.shape[1]
+    slots = one_ref.shape[0]
+    greet((("shard", shards), ("owner", owners)))
+
+    def at_shard(d):
+        return lax.rem(s_me + d, shards)
+
+    def from_shard(d):
+        return lax.rem(s_me - d + shards, shards)
+
+    def at_owner(d):
+        return lax.rem(o_me + d, owners)
+
+    def from_owner(d):
+        return lax.rem(o_me - d + owners, owners)
+
+    def rows(c):
+        return slice(c * chunk, (c + 1) * chunk)
+
+    own_pj = pltpu.make_async_copy(pj_ref.at[s_me], pj1.at[s_me], own_sem.at[CHUNKS])
+    own_pj.start()
+    own_pn = [pltpu.make_async_copy(pn_ref.at[s_me, rows(c)], pn1[c].at[s_me], own_sem.at[c]) for c in range(CHUNKS)]
+
+    @pl.loop(1, shards)
+    def _(d):
+        t = at_shard(d)
+        remote(pj_ref.at[t], pj1.at[s_me], j_send.at[d], j_recv.at[d], "shard", t).start()
+
+    for c in range(CHUNKS):
+        own_pn[c].start()
+
+        @pl.loop(1, shards)
+        def _(d):
+            t = at_shard(d)
+            remote(pn_ref.at[t, rows(c)], pn1[c].at[s_me], p_send.at[c, d], p_recv.at[c, d], "shard", t).start()
+
+    own_pj.wait()
+
+    @pl.loop(1, shards)
+    def _(d):
+        remote(pj_ref.at[at_shard(d)], pj1.at[from_shard(d)], j_send.at[d], j_recv.at[d], "shard", at_shard(d)).wait()
+
+    @pl.loop(1, owners)
+    def _(d):
+        t = at_owner(d)
+        pj_stage[t] = pj1[expert_ref[t]]
+        remote(pj_stage.at[t], pj2.at[o_me], jo_send.at[d], jo_recv.at[d], "owner", t).start()
+
+    pj2[o_me] = pj1[expert_ref[o_me]]
+
+    for c in range(CHUNKS):
+        own_pn[c].wait()
+
+        @pl.loop(1, shards)
+        def _(d):
+            t = at_shard(d)
+            remote(pn_ref.at[t, rows(c)], pn1[c].at[from_shard(d)], p_send.at[c, d], p_recv.at[c, d], "shard", t).wait()
+
+        @pl.loop(1, owners)
+        def _(d):
+            t = at_owner(d)
+            pn_stage[c, t] = pn1[c][expert_ref[t]]
+            remote(pn_stage.at[c, t], pn2[c].at[o_me], po_send.at[c, d], po_recv.at[c, d], "owner", t).start()
+
+        pn2[c][o_me] = pn1[c][expert_ref[o_me]]
+
+    @pl.loop(1, owners)
+    def _(d):
+        remote(pj_stage.at[at_owner(d)], pj2.at[from_owner(d)], jo_send.at[d], jo_recv.at[d], "owner", at_owner(d)).wait()
+
+    @pl.loop(0, slots)
+    def _(j):
+        projected = pj2[home_ref[j]]
+        one = BETA_ONE * one_ref[j] + (1.0 - BETA_ONE) * projected
+        two = BETA_TWO * two_ref[j] + (1.0 - BETA_TWO) * projected * projected
+        one_out[j] = one
+        two_out[j] = two
+        normed[s_me, j] = one / (jnp.sqrt(two) + EPSILON)
+
+    other = s_me + 1 - 2 * lax.rem(s_me, 2)
+    chips = shards // 2
+
+    @pl.loop(1, chips)
+    def _(k):
+        t = at_shard(2 * k)
+        remote(normed.at[s_me], normed.at[s_me], n_send.at[k], n_recv.at[k], "shard", t).start()
+
+    remote(normed.at[s_me], normed.at[s_me], f_send.at[0], f_recv.at[0], "shard", other).start()
+
+    @pl.loop(1, chips)
+    def _(k):
+        f = from_shard(2 * k)
+        remote(normed.at[s_me], normed.at[f], n_send.at[k], n_recv.at[k], "shard", at_shard(2 * k)).wait()
+        remote(normed.at[f], normed.at[f], f_send.at[k], f_recv.at[k], "shard", other).start()
+
+    @pl.loop(0, chips)
+    def _(k):
+        f = from_shard(2 * k)
+        g = lax.rem(other - 2 * k + shards, shards)
+        remote(normed.at[f], normed.at[g], f_send.at[k], f_recv.at[k], "shard", other).wait()
+
+    @pl.loop(0, slots)
+    def _(j):
+        h, l = split(normed[:, j].reshape(nh.shape[1], nh.shape[2]))
+        nh[j] = h
+        nl[j] = l
+
+    for c in range(CHUNKS):
+
+        @pl.loop(1, owners)
+        def _(d):
+            t = at_owner(d)
+            remote(pn_stage.at[c, t], pn2[c].at[from_owner(d)], po_send.at[c, d], po_recv.at[c, d], "owner", t).wait()
+
+        @pl.loop(0, slots)
+        def _(j):
+            b = pn2[c][home_ref[j]]
+            basis_out[j, rows(c)] = b
+            update_out[j, rows(c)] = (GALORE_SCALE * dot3(split(b), (nh[j], nl[j]), NN)).astype(BF)
+
+
+def leave(expert_for, home, pn, pj, one, two):
+    shards, rows, rank = pn.shape
+    part, cols = pj.shape[1:]
+    slots = one.shape[0]
+    owners = expert_for.shape[0]
+    chunk = rows // CHUNKS
+    dma = pltpu.SemaphoreType.DMA
+    smem = pl.BlockSpec(memory_space=pltpu.SMEM)
+    vmem = pl.BlockSpec(memory_space=V)
+    hbm = pl.BlockSpec(memory_space=pl.ANY)
     return pl.pallas_call(
-        update_body,
-        grid=(slots,),
-        out_shape=jax.ShapeDtypeStruct((slots, rows, cols), BF),
-        in_specs=[
-            pl.BlockSpec((1, rows, rank), lambda i: (i, 0, 0)),
-            pl.BlockSpec((1, rank, cols), lambda i: (i, 0, 0)),
+        functools.partial(leave_body, shards, owners),
+        out_shape=(
+            jax.ShapeDtypeStruct((slots, rows, rank), F32),
+            jax.ShapeDtypeStruct(one.shape, F32),
+            jax.ShapeDtypeStruct(two.shape, F32),
+            jax.ShapeDtypeStruct((slots, rows, cols), BF),
+        ),
+        in_specs=[smem, smem, hbm, hbm, vmem, vmem],
+        out_specs=(vmem,) * 4,
+        scratch_shapes=[
+            V((shards, part, cols), F32), V((owners, part, cols), F32), V((owners, part, cols), F32),
+            V((shards, chunk, rank), F32), V((shards, chunk, rank), F32), V((CHUNKS, owners, chunk, rank), F32),
+            V((owners, chunk, rank), F32), V((owners, chunk, rank), F32),
+            V((shards, slots, part, cols), F32), V((slots, rank, cols), BF), V((slots, rank, cols), BF),
+            dma((shards,)), dma((shards,)), dma((owners,)), dma((owners,)),
+            dma((CHUNKS, shards)), dma((CHUNKS, shards)), dma((CHUNKS, owners)), dma((CHUNKS, owners)),
+            dma((shards // 2,)), dma((shards // 2,)), dma((shards // 2,)), dma((shards // 2,)), dma((CHUNKS + 1,)),
         ],
-        out_specs=pl.BlockSpec((1, rows, cols), lambda i: (i, 0, 0)),
-        compiler_params=pltpu.CompilerParams(vmem_limit_bytes=32 * 1024 * 1024),
-        name="update",
-    )(basis, normed)
-
-
-def pick(array, index):
-    return jnp.stack([lax.dynamic_index_in_dim(array, index[i], 0, keepdims=False) for i in range(index.shape[0])])
+        compiler_params=pltpu.CompilerParams(
+            collective_id=1, has_side_effects=True, vmem_limit_bytes=56 * 1024 * 1024
+        ),
+        name="leave",
+    )(expert_for, home, pn, pj, one, two)
 
 
 def on_device(gradient, old_basis, moment_one, moment_two, slot_expert, cost):
@@ -348,17 +489,7 @@
 
     gh, gl, kh, kl, z, whole = enter(slot_for, holder, gradient, old_basis)
     basis, projected = refresh(count, gh, gl, kh, kl, z, whole)
-    result = jnp.concatenate([basis] + [projected[:, :, 256 * c : 256 * c + 256] for c in range(3)], axis=1)
-    result = lax.all_to_all(result, "shard", split_axis=0, concat_axis=0, tiled=True)
-    result = lax.all_to_all(pick(result, expert_for), "owner", split_axis=0, concat_axis=0, tiled=True)
-    result = pick(result, mine // slots)
-    basis_slot = result[:, :256, :]
-    projected = jnp.concatenate([result[:, 256 + 32 * c : 288 + 32 * c, :] for c in range(3)], axis=2)
-    moment_new = BETA_ONE * moment_one + (1.0 - BETA_ONE) * projected
-    second_new = BETA_TWO * moment_two + (1.0 - BETA_TWO) * projected * projected
-    normed = moment_new / (jnp.sqrt(second_new) + EPSILON)
-    update = make_update(basis_slot, lax.all_gather(normed, "shard", axis=1, tiled=True))
-    return (basis_slot, moment_new, second_new, update)
+    return tuple(leave(expert_for, mine // slots, basis, projected, moment_one, moment_two))
 
 
 def solution(mesh):

time: 398 us -> 293 us (0.74)
  Pallas kernels: 122 us -> 280 us
  waiting for transfers between devices: 111 us -> 0 us
  starting transfers between devices: 65.8 us -> 0 us
  between operations: 59.8 us -> 0.7 us
  local copies, waits for them, and re-layouts: 31.5 us -> 9.9 us
  other arithmetic: 6.47 us -> 1.97 us
    pallas_call x1, Pallas kernels: 5.44 us -> 164 us  [leave(): pl.pallas_call(functools.partial(leave_body, shards, owners), out_shape=(...]
    all_to_all x2 -> x0, waiting for transfers between devices: 72.4 us -> none  [the longest x1 68.3 us: on_device(): lax.all_to_all(pick(result, expert_for), 'owner', split_axis=0, concat_ax...]
    all_to_all x2 -> x0, starting transfers between devices: 65.7 us -> none  [the longest x1 52.1 us: on_device(): lax.all_to_all(pick(result, expert_for), 'owner', split_axis=0, concat_ax...]
    all_gather x1 -> x0, waiting for transfers between devices: 38.6 us -> none  [on_device(): lax.all_gather(normed, 'shard', axis=1, tiled=True)]
    unnamed x32 -> x8, local copies, waits for them, and re-layouts: 23.2 us -> 7.82 us
    slice x5 -> x0, local copies, waits for them, and re-layouts: 4.44 us -> none  [the longest x1 1.82 us: on_device(): basis_slot = result[:, :256, :]]
  transfers between devices with their start and end apart: 3 -> 0, of which waited for: 3 -> 0; matrix products, arithmetic and copies ran while one was open for 1% -> 0% of each run, Pallas kernels for 0% -> 0%
where the time goes in v3:
time: 293 us; the launch traced here: 292 us
  Pallas kernels  280 us (96%)
  local copies, waits for them, and re-layouts  9.9 us (3%)
    pallas_call x1, Pallas kernels, leave(): pl.pallas_call(functools.partial(leave_body, shards, owners), out_shape=(...  164 us
    pallas_call x1, Pallas kernels, enter(): pl.pallas_call(functools.partial(enter_body, shards, owners), out_shape=(...  109 us
    unnamed x8, local copies, waits for them, and re-layouts  7.82 us
    pallas_call x1, Pallas kernels, refresh(): pl.pallas_call(body, out_shape=(jax.ShapeDtypeStruct((shards, rows, rank)...  7.73 us

profile of v3, /device:TPU:1, one launch (start us, length us, event | category | flops | bytes accessed | tf_op | source)
XLA Modules:
  0.0 292.5 jit_solution(15026725491479866848)
XLA Ops:
  0.6 1.3 dynamic_slice.8.cnt
  1.9 0.7 eq.30
  2.7 0.5 and_select_fusion.1.home_ref
  3.2 0.1 copy.10
  3.3 0.8 fusion.1
  4.1 0.6 select_reduce_fusion.slot_ref
  4.7 108.5 %enter.1 = (bf16[8,256,768]{2,1,0:T(8,128)(2,1)}, bf16[8,256,768]{2,1,0:T(8,128)(2,1)}, bf16[768,768]{1,0:T(8,128)(2,1)}, bf16[768,768]{1,0:T(8,128)(2,1)}, f32[768,256]{1,0:T(8,128)}, /*index=5*/f32[8,256,256]{2,1,0:T(8,128)}) custom-call(s32[16]{0:T(128)} %select_reduce_fusion.slot_ref, s32[8]{0:T(128)} %get-tuple-element.20.holder_ref, ...), custom_call_target="tpu_custom_call" | custom-call | tf_op jit(solution)/shard_map/enter/pallas_call | solution.py:209
  113.2 7.7 %refresh.1 = (f32[8,256,256]{2,1,0:T(8,128)}, f32[8,32,768]{2,1,0:T(8,128)}) custom-call(s32[1]{0:T(128)} %dynamic_slice.8.cnt, bf16[8,256,768]{2,1,0:T(8,128)(2,1)} %get-tuple-element.12.gh_hbm, bf16[8,256,768]{2,1,0:T(8,128)(2,1)} %get-tuple-element.13.gl_hbm, bf16[768,768]{1,0:T(8,128)(2,1)} %get-tuple-element.14.kh_ref, ...), custom_call_target="tpu_custom_call" | custom-call | tf_op jit(solution)/shard_map/refresh/pallas_call | solution.py:286
  121.0 163.7 %leave.1 = (f32[8,256,256]{2,1,0:T(8,128)}, f32[8,32,768]{2,1,0:T(8,128)}, f32[8,32,768]{2,1,0:T(8,128)}, bf16[8,256,768]{2,1,0:T(8,128)(2,1)}) custom-call(s32[16]{0:T(128)} %get-tuple-element.21.expert_ref, s32[8]{0:T(128)} %and_select_fusion.1.home_ref, f32[8,256,256]{2,1,0:T(8,128)} %get-tuple-element.18.pn_ref, f32[8,32,768]{2,1,0:T(8,128)} %get-tuple-element.19.pj_ref, ...), custom_call_target="tpu_custom_call" | custom-call | tf_op jit(solution)/shard_map/leave/pallas_call | solution.py:449
  284.6 0.0 copy-start.1
  284.6 0.0 copy-start
  284.6 3.2 %copy.15 = f32[8,256,256]{2,1,0:T(8,128)} copy(f32[8,256,256]{2,1,0:T(8,128)} %get-tuple-element.26) | data formatting | bytes 4194304
  287.8 2.1 copy.16
  289.9 0.0 copy-done.1
  289.9 0.9 copy.17
  290.8 0.0 copy-done
  290.8 1.7 copy.18
  (2 shorter events, 0.0 us)
Async XLA Ops:
  284.6 5.3 %copy-start.1 = (f32[8,32,768]{2,1,0:T(8,128)S(1)}, f32[8,32,768]{2,1,0:T(8,128)}, u32[]{:S(2)}) copy-start(f32[8,32,768]{2,1,0:T(8,128)} %get-tuple-element.28) | copy-start | bytes 2359300
  284.6 6.2 %copy-start = (bf16[8,256,768]{2,1,0:T(8,128)(2,1)S(1)}, bf16[8,256,768]{2,1,0:T(8,128)(2,1)}, u32[]{:S(2)}) copy-start(bf16[8,256,768]{2,1,0:T(8,128)(2,1)} %get-tuple-element.29) | copy-start | bytes 9437188

commit v4 on v3

v4 whole, which is shorter than its diff:
```python
import functools
import jax, jax.numpy as jnp
from jax import lax
from jax.experimental import pallas as pl
from jax.sharding import PartitionSpec as P
from jax.experimental.pallas import tpu as pltpu

BF = jnp.bfloat16
F32 = jnp.float32

def split(x):
    hi = x.astype(BF)
    return hi, (x - hi.astype(F32)).astype(BF)

def mm(a, b, dims):
    return lax.dot_general(a, b, (dims, ((), ())), preferred_element_type=F32)

NN = ((1,), (0,))
TN = ((0,), (0,))
NT = ((1,), (1,))

def dot3(a, b, dims):
    ah, al = a
    bh, bl = b
    return mm(ah, bh, dims) + (mm(ah, bl, dims) + mm(al, bh, dims))

PANEL, GROUP = 32, 16


def factor(c_ref, xh, xl, ls, rs):
    nb, sub_nb = PANEL, GROUP
    n = c_ref.shape[0]
    for p in range(n // nb):
        lo = p * nb
        need = [h for h in range(4) if (h < 2 and h * 128 + 128 > lo) or (h >= 2 and (h - 2) * 128 < lo + nb)]
        sub = lax.broadcasted_iota(jnp.int32, (nb, 128), 0)
        s = {}
        for h in need:
            if h < 2:
                s[h] = c_ref[lo:lo + nb, 128 * h:128 * h + 128]
            else:
                l = lax.broadcasted_iota(jnp.int32, (nb, 128), 1) + 128 * (h - 2)
                s[h] = jnp.where(l == sub + lo, 1.0, 0.0)
        a0, a1 = need[0] * 128, need[-1] * 128 + 128
        cuts = []
        if p > 1:
            cuts.append((0, 3 * (lo - nb)))
        if p > 0:
            cuts.append((3 * (lo - nb), 3 * lo))
        for (x, y) in cuts:
            d = mm(ls[x:y, lo:lo + nb], rs[x:y, a0:a1], TN)
            for h in need:
                s[h] = s[h] - d[:, 128 * h - a0:128 * h - a0 + 128]
        hd = lo // 128
        off = lo - hd * 128
        pivots = []
        done = []
        for g in range(nb // sub_nb):
            b = g * sub_nb
            rows = nb - b
            rsub = lax.broadcasted_iota(jnp.int32, (rows, 128), 0)
            cols = [jnp.broadcast_to(s[hd][:, off + b + k:off + b + k + 1], (rows, 128)) for k in range(sub_nb)]
            for j in range(sub_nb):
                d = cols[j][j:j + 1, :]
                r = 1.0 / d
                pivots.append(d)
                m = jnp.where(rsub > j, cols[j] * r, 0.0)
                for k in range(j + 1, sub_nb):
                    cols[k] = cols[k] - m * cols[k][j:j + 1, :]
                for h in need:
                    s[h] = s[h] - m * s[h][j:j + 1, :]
            done.append({h: s[h][0:sub_nb] for h in need})
            if rows > sub_nb:
                s = {h: s[h][sub_nb:] for h in need}
        scale = lax.rsqrt(jnp.concatenate(pivots, axis=0))
        for h in range(4):
            if h not in need:
                o = jnp.zeros((nb, 128), F32)
            else:
                o = jnp.concatenate([t[h] for t in done], axis=0) * scale
                if h == hd:
                    l = lax.broadcasted_iota(jnp.int32, (nb, 128), 1) + 128 * h
                    o = jnp.where(l >= sub + lo, o, 0.0)
            cs = slice(128 * h, 128 * h + 128)
            hi = o.astype(BF)
            lw = (o - hi.astype(F32)).astype(BF)
            if h >= 2:
                xs = slice(128 * (h - 2), 128 * (h - 2) + 128)
                xh[lo:lo + nb, xs] = hi
                xl[lo:lo + nb, xs] = lw
            b = 3 * lo
            rs[b:b + nb, cs] = hi
            rs[b + nb:b + 2 * nb, cs] = lw
            rs[b + 2 * nb:b + 3 * nb, cs] = hi
            if h < 2:
                ls[b:b + nb, cs] = hi
                ls[b + nb:b + 2 * nb, cs] = hi
                ls[b + 2 * nb:b + 3 * nb, cs] = lw


MESH = pl.DeviceIdType.MESH
V = pltpu.VMEM


def greet(groups):
    barrier = pltpu.get_barrier_semaphore()
    total = 0
    for axis, size in groups:
        me = lax.axis_index(axis)

        @pl.loop(1, size)
        def _(d):
            pl.semaphore_signal(barrier, inc=1, device_id={axis: lax.rem(me + d, size)}, device_id_type=MESH)

        total += size - 1
    pl.semaphore_wait(barrier, total)


def remote(src, dst, send, recv, axis, target):
    return pltpu.make_async_remote_copy(
        src_ref=src, dst_ref=dst, send_sem=send, recv_sem=recv, device_id={axis: target}, device_id_type=MESH
    )


def slot_at(table, owner, slots, home):
    found = 0
    for j in range(slots):
        found = jnp.where(lax.div(table[owner * slots + j], slots) == home, j, found)
    return found


def enter_body(shards, owners, table, g_ref, b_ref, gh_out, gl_out, kh_out, kl_out, z_out, p_out,
               gland, gh, gl, kacc, kh, kl, stage, landed, stage2, pland,
               g_send, g_recv, a_send, a_recv, b_send, b_recv, own_sem, h_sem, l_sem, p_sem, k_sem):
    s_me = lax.axis_index("shard")
    o_me = lax.axis_index("owner")
    greet((("shard", shards), ("owner", owners)))

    def at_shard(d):
        return lax.rem(s_me + d, shards)

    def from_shard(d):
        return lax.rem(s_me - d + shards, shards)

    def at_owner(d):
        return lax.rem(o_me + d, owners)

    def from_owner(d):
        return lax.rem(o_me - d + owners, owners)

    own = pltpu.make_async_copy(g_ref.at[s_me], gland.at[s_me], own_sem)
    own.start()

    slots = shards

    @pl.loop(1, owners)
    def _(d):
        t = at_owner(d)
        stage[t] = b_ref[slot_at(table, o_me, slots, t)]
        remote(stage.at[t], landed.at[o_me], a_send.at[d], a_recv.at[d], "owner", t).start()

    @pl.loop(1, shards)
    def _(d):
        t = at_shard(d)
        remote(g_ref.at[t], gland.at[s_me], g_send.at[d], g_recv.at[d], "shard", t).start()

    landed[o_me] = b_ref[slot_at(table, o_me, slots, o_me)]
    kacc[...] = jnp.zeros_like(kacc)
    own.wait()
    tiles = kacc.shape[0] // 256

    def gram(f):
        h, l = split(gland[f])
        gh[f] = h
        gl[f] = l
        pltpu.make_async_copy(gh.at[f], gh_out.at[f], h_sem.at[f]).start()
        pltpu.make_async_copy(gl.at[f], gl_out.at[f], l_sem.at[f]).start()
        for a in range(tiles):
            ra = slice(256 * a, 256 * a + 256)
            for b in range(a, tiles):
                rb = slice(256 * b, 256 * b + 256)
                kacc[ra, rb] += dot3((h[:, ra], l[:, ra]), (h[:, rb], l[:, rb]), TN)

    gram(s_me)

    def take_gram(d):
        f = from_shard(d)
        remote(g_ref.at[at_shard(d)], gland.at[f], g_send.at[d], g_recv.at[d], "shard", at_shard(d)).wait_recv()
        gram(f)

    half = EARLY
    pl.loop(1, half)(take_gram)

    @pl.loop(1, owners)
    def _(d):
        remote(stage.at[at_owner(d)], landed.at[from_owner(d)], a_send.at[d], a_recv.at[d], "owner", at_owner(d)).wait()

    def holder(i):
        def add(o, found):
            for j in range(slots):
                found = jnp.where(table[o * slots + j] == o_me * slots + i, o, found)
            return found

        return lax.fori_loop(0, owners, add, 0)

    @pl.loop(1, shards)
    def _(d):
        t = at_shard(d)
        stage2[t] = landed[holder(t)]
        remote(stage2.at[t], pland.at[s_me], b_send.at[d], b_recv.at[d], "shard", t).start()

    pland[s_me] = landed[holder(s_me)]
    pl.loop(half, shards)(take_gram)

    for a in range(tiles):
        ra = slice(256 * a, 256 * a + 256)
        for b in range(a, tiles):
            rb = slice(256 * b, 256 * b + 256)
            h, l = split(kacc[ra, rb])
            kh[ra, rb] = h
            kl[ra, rb] = l
            if b > a:
                h, l = split(kacc[ra, rb].T)
                kh[rb, ra] = h
                kl[rb, ra] = l

    save_k = (pltpu.make_async_copy(kh, kh_out, k_sem.at[0]), pltpu.make_async_copy(kl, kl_out, k_sem.at[1]))
    for copy in save_k:
        copy.start()

    def project(f):
        pltpu.make_async_copy(pland.at[f], p_out.at[f], p_sem.at[f]).start()
        return dot3((gh[f], gl[f]), split(pland[f]), TN)

    z_out[...] = project(s_me)

    @pl.loop(1, shards)
    def _(d):
        f = from_shard(d)
        remote(stage2.at[at_shard(d)], pland.at[f], b_send.at[d], b_recv.at[d], "shard", at_shard(d)).wait()
        z_out[...] += project(f)

    @pl.loop(1, shards)
    def _(d):
        remote(g_ref.at[at_shard(d)], gland.at[from_shard(d)], g_send.at[d], g_recv.at[d], "shard", at_shard(d)).wait_send()

    @pl.loop(0, shards)
    def _(f):
        pltpu.make_async_copy(gh.at[f], gh_out.at[f], h_sem.at[f]).wait()
        pltpu.make_async_copy(gl.at[f], gl_out.at[f], l_sem.at[f]).wait()
        pltpu.make_async_copy(pland.at[f], p_out.at[f], p_sem.at[f]).wait()

    for copy in save_k:
        copy.wait()


EARLY = 5


def enter(table, gradient, basis):
    shards, rows, cols = gradient.shape
    rank = basis.shape[2]
    owners = table.shape[0] // basis.shape[0]
    sem = pltpu.SemaphoreType.DMA
    smem = pl.BlockSpec(memory_space=pltpu.SMEM)
    vmem = pl.BlockSpec(memory_space=V)
    hbm = pl.BlockSpec(memory_space=pl.ANY)
    return pl.pallas_call(
        functools.partial(enter_body, shards, owners),
        out_shape=(
            jax.ShapeDtypeStruct((shards, rows, cols), BF),
            jax.ShapeDtypeStruct((shards, rows, cols), BF),
            jax.ShapeDtypeStruct((cols, cols), BF),
            jax.ShapeDtypeStruct((cols, cols), BF),
            jax.ShapeDtypeStruct((cols, rank), F32),
            jax.ShapeDtypeStruct((shards, rows, rank), F32),
        ),
        in_specs=[smem, hbm, vmem],
        out_specs=(hbm, hbm, hbm, hbm, vmem, hbm),
        scratch_shapes=[
            V((shards, rows, cols), F32), V((shards, rows, cols), BF), V((shards, rows, cols), BF), V((cols, cols), F32), V((cols, cols), BF), V((cols, cols), BF),
            V((owners, rows, rank), F32), V((owners, rows, rank), F32), V((shards, rows, rank), F32), V((shards, rows, rank), F32),
            sem((shards,)), sem((shards,)), sem((owners,)), sem((owners,)), sem((shards,)), sem((shards,)),
            sem, sem((shards,)), sem((shards,)), sem((shards,)), sem((2,)),
        ],
        compiler_params=pltpu.CompilerParams(
            collective_id=0, has_side_effects=True, vmem_limit_bytes=56 * 1024 * 1024
        ),
        name="enter",
    )(table, gradient, basis)


def body(table, cost, kh_ref, kl_ref, zin_ref, mh_ref, ml_ref, pj_ref, keep_ref, home_ref, z_ref, w_ref, c_ref, xh, xl, ls, rs):
    s_me = lax.axis_index("shard")
    o_me = lax.axis_index("owner")
    shards, part, cols = pj_ref.shape
    rank = zin_ref.shape[1]
    count = cost[o_me * shards + s_me]
    keep_ref[0] = jnp.where(count > 0, 0.0, 1.0)
    for j in range(shards):
        home_ref[j] = lax.div(table[o_me * shards + j], shards)
    z_ref[...] = zin_ref[...]

    @pl.loop(0, count)
    def _(it):
        z = split(z_ref[...])
        w_ref[...] = dot3((kh_ref[...], kl_ref[...]), z, NN)
        w = split(w_ref[...])
        c_ref[...] = dot3(z, w, TN)
        factor(c_ref, xh, xl, ls, rs)
        x = (xh[...], xl[...])
        z_ref[...] = dot3(w, x, NT)

        @pl.when(it == count - 1)
        def _():
            h, l = split(dot3(z, x, NT))
            mh_ref[...] = h
            ml_ref[...] = l

    @pl.when(count == 0)
    def _():
        mh_ref[...] = jnp.zeros_like(mh_ref)
        ml_ref[...] = jnp.zeros_like(ml_ref)

    for c in range(cols // 256):
        t = z_ref[256 * c:256 * c + 256, :].T
        for s in range(shards):
            pj_ref[s, :, 256 * c:256 * c + 256] = t[part * s:part * s + part, :]


def refresh(table, cost, shards, kh, kl, z):
    cols, rank = z.shape
    smem = pl.BlockSpec(memory_space=pltpu.SMEM)
    vmem = pl.BlockSpec(memory_space=V)
    return pl.pallas_call(
        body,
        out_shape=(
            jax.ShapeDtypeStruct((cols, rank), BF),
            jax.ShapeDtypeStruct((cols, rank), BF),
            jax.ShapeDtypeStruct((shards, rank // shards, cols), F32),
            jax.ShapeDtypeStruct((1,), F32),
            jax.ShapeDtypeStruct((shards,), jnp.int32),
        ),
        in_specs=[smem, smem, vmem, vmem, vmem],
        out_specs=(vmem, vmem, vmem, smem, smem),
        scratch_shapes=[
            V((cols, rank), F32), V((cols, rank), F32), V((rank, rank), F32), V((rank, rank), BF), V((rank, rank), BF),
            V((3 * rank, rank), BF), V((3 * rank, 2 * rank), BF),
        ],
        compiler_params=pltpu.CompilerParams(vmem_limit_bytes=56 * 1024 * 1024),
        name="refresh",
    )(table, cost, kh, kl, z)


BETA_ONE = 0.9
BETA_TWO = 0.99
EPSILON = 1e-08
GALORE_SCALE = 0.25
CHUNKS = 2


def adam(one, two, projected):
    one = BETA_ONE * one + (1.0 - BETA_ONE) * projected
    two = BETA_TWO * two + (1.0 - BETA_TWO) * projected * projected
    return one, two


def leave_body(shards, owners, table, keep_ref, mh_ref, ml_ref, pj_ref, gh_hbm, gl_hbm, p_hbm, one_ref, two_ref,
               back_a, back_b, normed_out, proj_out,
               gh, gl, p_in, pn, pj1, pj_stage, pj2, pn1a, pn1b, pn_stage, normed,
               h_sem, l_sem, i_sem, j_send, j_recv, jo_send, jo_recv, p_send, p_recv, po_send, po_recv,
               n_send, n_recv, f_send, f_recv, own_sem):
    s_me = lax.axis_index("shard")
    o_me = lax.axis_index("owner")
    slots = one_ref.shape[0]
    pn1, back = (pn1a, pn1b), (back_a, back_b)
    chunk = pn1a.shape[1]

    def at_shard(d):
        return lax.rem(s_me + d, shards)

    def from_shard(d):
        return lax.rem(s_me - d + shards, shards)

    def at_owner(d):
        return lax.rem(o_me + d, owners)

    def from_owner(d):
        return lax.rem(o_me - d + owners, owners)

    def rows(c):
        return slice(c * chunk, (c + 1) * chunk)

    def loads(t):
        return (
            pltpu.make_async_copy(gh_hbm.at[t], gh.at[t], h_sem.at[t]),
            pltpu.make_async_copy(gl_hbm.at[t], gl.at[t], l_sem.at[t]),
            pltpu.make_async_copy(p_hbm.at[t], p_in.at[t], i_sem.at[t]),
        )

    @pl.loop(1, shards + 1)
    def _(d):
        for copy in loads(at_shard(d)):
            copy.start()

    greet((("shard", shards), ("owner", owners)))

    @pl.loop(1, shards)
    def _(d):
        t = at_shard(d)
        remote(pj_ref.at[t], pj1.at[s_me], j_send.at[d], j_recv.at[d], "shard", t).start()

    pj1[s_me] = pj_ref[s_me]
    keep = keep_ref[0]

    def basis_rows(t, c):
        return dot3((gh[t, rows(c)], gl[t, rows(c)]), (mh_ref[...], ml_ref[...]), NN) + keep * p_in[t, rows(c)]

    for c in range(CHUNKS):

        @pl.loop(1, shards)
        def _(d):
            t = at_shard(d)
            if c == 0:
                for copy in loads(t):
                    copy.wait()
            pn[c, t] = basis_rows(t, c)
            remote(pn.at[c, t], pn1[c].at[s_me], p_send.at[c, d], p_recv.at[c, d], "shard", t).start()

        if c == 0:
            for copy in loads(s_me):
                copy.wait()
        pn1[c][s_me] = basis_rows(s_me, c)

    def expert_at(owner):
        found = 0
        for j in range(slots):
            e = table[owner * slots + j]
            found = jnp.where(lax.div(e, slots) == o_me, lax.rem(e, slots), found)
        return found

    @pl.loop(1, shards)
    def _(d):
        remote(pj_ref.at[at_shard(d)], pj1.at[from_shard(d)], j_send.at[d], j_recv.at[d], "shard", at_shard(d)).wait()

    @pl.loop(1, owners)
    def _(d):
        t = at_owner(d)
        pj_stage[t] = pj1[expert_at(t)]
        remote(pj_stage.at[t], pj2.at[o_me], jo_send.at[d], jo_recv.at[d], "owner", t).start()

    pj2[o_me] = pj1[expert_at(o_me)]
    own = []
    for c in range(CHUNKS):

        @pl.loop(1, shards)
        def _(d):
            t = at_shard(d)
            remote(pn.at[c, t], pn1[c].at[from_shard(d)], p_send.at[c, d], p_recv.at[c, d], "shard", t).wait()

        @pl.loop(1, owners)
        def _(d):
            t = at_owner(d)
            pn_stage[c, t] = pn1[c][expert_at(t)]
            remote(pn_stage.at[c, t], back[c].at[o_me], po_send.at[c, d], po_recv.at[c, d], "owner", t).start()

        pn_stage[c, o_me] = pn1[c][expert_at(o_me)]
        own.append(pltpu.make_async_copy(pn_stage.at[c, o_me], back[c].at[o_me], own_sem.at[c]))
        own[-1].start()

    @pl.loop(1, owners)
    def _(d):
        remote(pj_stage.at[at_owner(d)], pj2.at[from_owner(d)], jo_send.at[d], jo_recv.at[d], "owner", at_owner(d)).wait()

    @pl.loop(0, slots)
    def _(j):
        projected = pj2[lax.div(table[o_me * slots + j], slots)]
        proj_out[j] = projected
        one, two = adam(one_ref[j], two_ref[j], projected)
        normed[j] = one / (jnp.sqrt(two) + EPSILON)

    other = s_me + 1 - 2 * lax.rem(s_me, 2)
    chips = shards // 2

    @pl.loop(1, chips)
    def _(k):
        t = at_shard(2 * k)
        remote(normed, normed_out.at[s_me], n_send.at[k], n_recv.at[k], "shard", t).start()

    remote(normed, normed_out.at[s_me], f_send.at[0], f_recv.at[0], "shard", other).start()
    own.append(pltpu.make_async_copy(normed, normed_out.at[s_me], own_sem.at[CHUNKS]))
    own[-1].start()

    @pl.loop(1, chips)
    def _(k):
        f = from_shard(2 * k)
        remote(normed, normed_out.at[f], n_send.at[k], n_recv.at[k], "shard", at_shard(2 * k)).wait()
        remote(normed_out.at[f], normed_out.at[f], f_send.at[k], f_recv.at[k], "shard", other).start()

    @pl.loop(0, chips)
    def _(k):
        g = lax.rem(other - 2 * k + shards, shards)
        remote(normed, normed_out.at[g], f_send.at[k], f_recv.at[k], "shard", other).wait()

    for copy in own:
        copy.wait()

    for c in range(CHUNKS):

        @pl.loop(1, owners)
        def _(d):
            t = at_owner(d)
            remote(pn_stage.at[c, t], back[c].at[from_owner(d)], po_send.at[c, d], po_recv.at[c, d], "owner", t).wait()


def leave(table, keep, mh, ml, pj, gh, gl, p, one, two):
    shards, rows, cols = gh.shape
    rank = p.shape[2]
    part = pj.shape[1]
    slots = one.shape[0]
    owners = table.shape[0] // slots
    chunk = rows // CHUNKS
    dma = pltpu.SemaphoreType.DMA
    smem = pl.BlockSpec(memory_space=pltpu.SMEM)
    vmem = pl.BlockSpec(memory_space=V)
    hbm = pl.BlockSpec(memory_space=pl.ANY)
    return pl.pallas_call(
        functools.partial(leave_body, shards, owners),
        out_shape=(
            jax.ShapeDtypeStruct((owners, chunk, rank), F32),
            jax.ShapeDtypeStruct((owners, chunk, rank), F32),
            jax.ShapeDtypeStruct((shards, slots, part, cols), F32),
            jax.ShapeDtypeStruct((slots, part, cols), F32),
        ),
        in_specs=[smem, smem, vmem, vmem, vmem, hbm, hbm, hbm, vmem, vmem],
        out_specs=(hbm, hbm, hbm, vmem),
        scratch_shapes=[
            V(gh.shape, BF), V(gh.shape, BF), V(p.shape, F32), V((CHUNKS, shards, chunk, rank), F32),
            V((shards, part, cols), F32), V((owners, part, cols), F32), V((owners, part, cols), F32),
            V((shards, chunk, rank), F32), V((shards, chunk, rank), F32), V((CHUNKS, owners, chunk, rank), F32),
            V((slots, part, cols), F32),
            dma((shards,)), dma((shards,)), dma((shards,)),
            dma((shards,)), dma((shards,)), dma((owners,)), dma((owners,)),
            dma((CHUNKS, shards)), dma((CHUNKS, shards)), dma((CHUNKS, owners)), dma((CHUNKS, owners)),
            dma((shards // 2,)), dma((shards // 2,)), dma((shards // 2,)), dma((shards // 2,)), dma((CHUNKS + 1,)),
        ],
        compiler_params=pltpu.CompilerParams(
            collective_id=1, has_side_effects=True, vmem_limit_bytes=56 * 1024 * 1024
        ),
        name="leave",
    )(table, keep, mh, ml, pj, gh, gl, p, one, two)


def finish_body(home_ref, back_a, back_b, normed_ref, proj_ref, one_ref, two_ref, basis_out, one_out, two_out, update_out):
    one_out[0], two_out[0] = adam(one_ref[0], two_ref[0], proj_ref[0])
    shards, _, part, cols = normed_ref.shape
    normed = split(normed_ref[:, 0].reshape(shards * part, cols))
    chunk = back_a.shape[1]
    for c, ref in enumerate((back_a, back_b)):
        at = slice(c * chunk, (c + 1) * chunk)
        basis_out[0, at] = ref[0]
        update_out[0, at] = (GALORE_SCALE * dot3(split(ref[0]), normed, NN)).astype(BF)


def finish(home, back_a, back_b, normed, projected, one, two):
    shards, slots, part, cols = normed.shape
    _, chunk, rank = back_a.shape
    small = pl.BlockSpec((1, part, cols), lambda j, home: (j, 0, 0))
    return pl.pallas_call(
        finish_body,
        out_shape=(
            jax.ShapeDtypeStruct((slots, 2 * chunk, rank), F32),
            jax.ShapeDtypeStruct(one.shape, F32),
            jax.ShapeDtypeStruct(two.shape, F32),
            jax.ShapeDtypeStruct((slots, 2 * chunk, cols), BF),
        ),
        grid_spec=pltpu.PrefetchScalarGridSpec(
            num_scalar_prefetch=1,
            grid=(slots,),
            in_specs=[
                pl.BlockSpec((1, chunk, rank), lambda j, home: (home[j], 0, 0)),
                pl.BlockSpec((1, chunk, rank), lambda j, home: (home[j], 0, 0)),
                pl.BlockSpec((shards, 1, part, cols), lambda j, home: (0, j, 0, 0)),
                small, small, small,
            ],
            out_specs=(
                pl.BlockSpec((1, 2 * chunk, rank), lambda j, home: (j, 0, 0)),
                small, small,
                pl.BlockSpec((1, 2 * chunk, cols), lambda j, home: (j, 0, 0)),
            ),
        ),
        compiler_params=pltpu.CompilerParams(vmem_limit_bytes=32 * 1024 * 1024),
        name="finish",
    )(home, back_a, back_b, normed, projected, one, two)


def on_device(gradient, old_basis, moment_one, moment_two, slot_expert, cost):
    gh, gl, kh, kl, z, p = enter(slot_expert, gradient, old_basis)
    mh, ml, pj, keep, home = refresh(slot_expert, cost, gradient.shape[0], kh, kl, z)
    back_a, back_b, normed, projected = leave(slot_expert, keep, mh, ml, pj, gh, gl, p, moment_one, moment_two)
    return tuple(finish(home, back_a, back_b, normed, projected, moment_one, moment_two))


def solution(mesh):
    spec = P("owner", "shard", None)
    return jax.shard_map(
        on_device, mesh=mesh, in_specs=(spec,) * 4 + (P(), P()), out_specs=(spec,) * 4, check_vma=False
    )
```

time: 293 us -> 267 us (0.911)
  Pallas kernels: 280 us -> 259 us
    pallas_call x1, Pallas kernels: 164 us -> 141 us  [leave(): pl.pallas_call(functools.partial(leave_body, shards, owners), out_shape=(...]
    pallas_call x1 -> x2, Pallas kernels: 7.73 us -> 10 us  [the longest x1 6.75 us: finish(): pl.pallas_call(finish_body, out_shape=(jax.ShapeDtypeStruct((slots, 2 * c...]
    unnamed x8 -> x14, local copies, waits for them, and re-layouts: 7.82 us -> 7.11 us
where the time goes in v4:
time: 267 us
  Pallas kernels  259 us (97%)
  local copies, waits for them, and re-layouts  7.11 us (3%)
    pallas_call x1, Pallas kernels, leave(): pl.pallas_call(functools.partial(leave_body, shards, owners), out_shape=(...  141 us
    pallas_call x1, Pallas kernels, enter(): pl.pallas_call(functools.partial(enter_body, shards, owners), out_shape=(...  108 us
    unnamed x14, local copies, waits for them, and re-layouts  7.11 us
    pallas_call x1, Pallas kernels, finish(): pl.pallas_call(finish_body, out_shape=(jax.ShapeDtypeStruct((slots, 2 * c...  6.75 us

profile of v4, /device:TPU:1, one launch (start us, length us, event | category | flops | bytes accessed | tf_op | source)
XLA Modules:
  0.0 266.8 jit_solution(15320979859913997621)
XLA Ops:
  0.6 107.5 %enter.1 = (bf16[8,256,768]{2,1,0:T(8,128)(2,1)}, bf16[8,256,768]{2,1,0:T(8,128)(2,1)}, bf16[768,768]{1,0:T(8,128)(2,1)}, bf16[768,768]{1,0:T(8,128)(2,1)}, f32[768,256]{1,0:T(8,128)}, /*index=5*/f32[8,256,256]{2,1,0:T(8,128)}) custom-call(s32[128]{0:T(128)} %table.5, f32[8,256,768]{2,1,0:T(8,128)} %g_ref.1, f32[8,256,256]{2,1,0:T(8,128)} %b_ref.1), custom_call_target="tpu_custom_call" | custom-call | tf_op jit(solution)/shard_map/enter/pallas_call | solution.py:268
  108.2 3.3 %refresh.1 = (bf16[768,256]{1,0:T(8,128)(2,1)}, bf16[768,256]{1,0:T(8,128)(2,1)}, f32[8,32,768]{2,1,0:T(8,128)}, f32[1]{0:T(128)}, s32[8]{0:T(128)}) custom-call(s32[128]{0:T(128)} %table.5, s32[128]{0:T(128)} %cost.1, bf16[768,768]{1,0:T(8,128)(2,1)} %get-tuple-element.19.kh_ref, bf16[768,768]{1,0:T(8,128)(2,1)} %get-tuple-element.20.kl_ref, ...), custom_call_target="tpu_custom_call" | custom-call | tf_op jit(solution)/shard_map/refresh/pallas_call | solution.py:335
  111.5 0.0 copy-start.1
  111.5 0.0 copy-start.2
  111.5 0.0 copy-start.6
  111.5 141.4 %leave.1 = (f32[16,128,256]{2,1,0:T(8,128)}, f32[16,128,256]{2,1,0:T(8,128)}, f32[8,8,32,768]{3,2,1,0:T(8,128)}, f32[8,32,768]{2,1,0:T(8,128)}) custom-call(s32[128]{0:T(128)} %table.5, f32[1]{0:T(128)} %get-tuple-element.23.keep_ref, bf16[768,256]{1,0:T(8,128)(2,1)} %get-tuple-element.24.mh_ref, bf16[768,256]{1,0:T(8,128)(2,1)} %get-tuple-element.25.ml_ref, ...), custom_call_target="tpu_custom_call" | custom-call | tf_op jit(solution)/shard_map/leave/pallas_call | solution.py:527
  252.9 0.0 copy-done.1
  252.9 0.0 copy-done.2
  252.9 0.0 copy-done.6
  252.9 0.0 copy-start
  252.9 2.8 %copy-done = f32[8,8,32,768]{3,2,1,0:T(8,128)S(1)} copy-done((f32[8,8,32,768]{3,2,1,0:T(8,128)S(1)}, f32[8,8,32,768]{3,2,1,0:T(8,128)}, u32[]{:S(2)}) %copy-start) | copy-done | bytes 6291480
  255.7 0.0 copy-start.3
  255.7 1.6 copy-done.3
  257.3 0.0 copy-start.4
  257.3 1.6 copy-done.4
  258.9 0.0 copy-start.5
  258.9 1.1 copy-done.5
  260.0 6.7 %finish.1 = (f32[8,256,256]{2,1,0:T(8,128)}, f32[8,32,768]{2,1,0:T(8,128)}, f32[8,32,768]{2,1,0:T(8,128)}, bf16[8,256,768]{2,1,0:T(8,128)(2,1)}) custom-call(s32[8]{0:T(128)S(1)} %copy-done.6, f32[16,128,256]{2,1,0:T(8,128)S(1)} %copy-done.3, f32[16,128,256]{2,1,0:T(8,128)S(1)} %copy-done.4, f32[8,8,32,768]{3,2,1,0:T(8,128)S(1)} %copy-done, ...), custom_call_target="tpu_custom_call" | custom-call | tf_op jit(solution)/shard_map/finish/pallas_call | solution.py:569
Async XLA Ops:
  111.5 141.4 %copy-start.1 = (f32[8,32,768]{2,1,0:T(8,128)S(1)}, f32[8,32,768]{2,1,0:T(8,128)}, u32[]{:S(2)}) copy-start(f32[8,32,768]{2,1,0:T(8,128)} %one_ref.3) | copy-start | bytes 2359300
  111.5 141.4 %copy-start.2 = (f32[8,32,768]{2,1,0:T(8,128)S(1)}, f32[8,32,768]{2,1,0:T(8,128)}, u32[]{:S(2)}) copy-start(f32[8,32,768]{2,1,0:T(8,128)} %two_ref.3) | copy-start | bytes 2359300
  111.5 141.4 %copy-start.6 = (s32[8]{0:T(128)S(1)}, s32[8]{0:T(128)}, u32[]{:S(2)}) copy-start(s32[8]{0:T(128)} %get-tuple-element.22.home_ref) | copy-start | bytes 100
  252.9 2.8 %copy-start = (f32[8,8,32,768]{3,2,1,0:T(8,128)S(1)}, f32[8,8,32,768]{3,2,1,0:T(8,128)}, u32[]{:S(2)}) copy-start(f32[8,8,32,768]{3,2,1,0:T(8,128)} %get-tuple-element.32.normed_ref) | copy-start | bytes 18874372
  255.7 1.6 copy-start.3
  257.3 1.6 copy-start.4
  258.9 1.1 copy-start.5

commit v5 on v4

--- a/solution.py
+++ b/solution.py
@@ -116,6 +116,20 @@
     pl.semaphore_wait(barrier, total)
 
 
+STEPS = (
+    (1, 1), (3, 3), (1, 3), (3, 1), (1, 0), (0, 1), (3, 0), (0, 3), (2, 0), (0, 2), (2, 2), (2, 1), (1, 2), (2, 3), (3, 2),
+)
+SIDE = 4
+
+
+def partners(me):
+    z, y = lax.div(me, SIDE), lax.rem(me, SIDE)
+    for k, (dy, dz) in enumerate(STEPS):
+        to = lax.rem(z + dz, SIDE) * SIDE + lax.rem(y + dy, SIDE)
+        source = lax.rem(z + SIDE - dz, SIDE) * SIDE + lax.rem(y + SIDE - dy, SIDE)
+        yield k, to, source
+
+
 def remote(src, dst, send, recv, axis, target):
     return pltpu.make_async_remote_copy(
         src_ref=src, dst_ref=dst, send_sem=send, recv_sem=recv, device_id={axis: target}, device_id_type=MESH
@@ -135,6 +149,7 @@
     s_me = lax.axis_index("shard")
     o_me = lax.axis_index("owner")
     greet((("shard", shards), ("owner", owners)))
+    slots = shards
 
     def at_shard(d):
         return lax.rem(s_me + d, shards)
@@ -142,27 +157,17 @@
     def from_shard(d):
         return lax.rem(s_me - d + shards, shards)
 
-    def at_owner(d):
-        return lax.rem(o_me + d, owners)
-
-    def from_owner(d):
-        return lax.rem(o_me - d + owners, owners)
-
     own = pltpu.make_async_copy(g_ref.at[s_me], gland.at[s_me], own_sem)
     own.start()
 
-    slots = shards
-
-    @pl.loop(1, owners)
-    def _(d):
-        t = at_owner(d)
-        stage[t] = b_ref[slot_at(table, o_me, slots, t)]
-        remote(stage.at[t], landed.at[o_me], a_send.at[d], a_recv.at[d], "owner", t).start()
-
     @pl.loop(1, shards)
     def _(d):
         t = at_shard(d)
         remote(g_ref.at[t], gland.at[s_me], g_send.at[d], g_recv.at[d], "shard", t).start()
+
+    for k, t, _ in partners(o_me):
+        stage[t] = b_ref[slot_at(table, o_me, slots, t)]
+        remote(stage.at[t], landed.at[o_me], a_send.at[k], a_recv.at[k], "owner", t).start()
 
     landed[o_me] = b_ref[slot_at(table, o_me, slots, o_me)]
     kacc[...] = jnp.zeros_like(kacc)
@@ -191,9 +196,8 @@
     half = EARLY
     pl.loop(1, half)(take_gram)
 
-    @pl.loop(1, owners)
-    def _(d):
-        remote(stage.at[at_owner(d)], landed.at[from_owner(d)], a_send.at[d], a_recv.at[d], "owner", at_owner(d)).wait()
+    for k, t, source in partners(o_me):
+        remote(stage.at[t], landed.at[source], a_send.at[k], a_recv.at[k], "owner", t).wait()
 
     def holder(i):
         def add(o, found):
@@ -382,12 +386,6 @@
     def from_shard(d):
         return lax.rem(s_me - d + shards, shards)
 
-    def at_owner(d):
-        return lax.rem(o_me + d, owners)
-
-    def from_owner(d):
-        return lax.rem(o_me - d + owners, owners)
-
     def rows(c):
         return slice(c * chunk, (c + 1) * chunk)
 
@@ -443,11 +441,9 @@
     def _(d):
         remote(pj_ref.at[at_shard(d)], pj1.at[from_shard(d)], j_send.at[d], j_recv.at[d], "shard", at_shard(d)).wait()
 
-    @pl.loop(1, owners)
-    def _(d):
-        t = at_owner(d)
+    for k, t, _ in partners(o_me):
         pj_stage[t] = pj1[expert_at(t)]
-        remote(pj_stage.at[t], pj2.at[o_me], jo_send.at[d], jo_recv.at[d], "owner", t).start()
+        remote(pj_stage.at[t], pj2.at[o_me], jo_send.at[k], jo_recv.at[k], "owner", t).start()
 
     pj2[o_me] = pj1[expert_at(o_me)]
     own = []
@@ -458,19 +454,16 @@
             t = at_shard(d)
             remote(pn.at[c, t], pn1[c].at[from_shard(d)], p_send.at[c, d], p_recv.at[c, d], "shard", t).wait()
 
-        @pl.loop(1, owners)
-        def _(d):
-            t = at_owner(d)
+        for k, t, _ in partners(o_me):
             pn_stage[c, t] = pn1[c][expert_at(t)]
-            remote(pn_stage.at[c, t], back[c].at[o_me], po_send.at[c, d], po_recv.at[c, d], "owner", t).start()
+            remote(pn_stage.at[c, t], back[c].at[o_me], po_send.at[c, k], po_recv.at[c, k], "owner", t).start()
 
         pn_stage[c, o_me] = pn1[c][expert_at(o_me)]
         own.append(pltpu.make_async_copy(pn_stage.at[c, o_me], back[c].at[o_me], own_sem.at[c]))
         own[-1].start()
 
-    @pl.loop(1, owners)
-    def _(d):
-        remote(pj_stage.at[at_owner(d)], pj2.at[from_owner(d)], jo_send.at[d], jo_recv.at[d], "owner", at_owner(d)).wait()
+    for k, t, source in partners(o_me):
+        remote(pj_stage.at[t], pj2.at[source], jo_send.at[k], jo_recv.at[k], "owner", t).wait()
 
     @pl.loop(0, slots)
     def _(j):
@@ -507,10 +500,8 @@
 
     for c in range(CHUNKS):
 
-        @pl.loop(1, owners)
-        def _(d):
-            t = at_owner(d)
-            remote(pn_stage.at[c, t], back[c].at[from_owner(d)], po_send.at[c, d], po_recv.at[c, d], "owner", t).wait()
+        for k, t, source in partners(o_me):
+            remote(pn_stage.at[c, t], back[c].at[source], po_send.at[c, k], po_recv.at[c, k], "owner", t).wait()
 
 
 def leave(table, keep, mh, ml, pj, gh, gl, p, one, two):
@@ -589,7 +580,7 @@
                 pl.BlockSpec((1, 2 * chunk, cols), lambda j, home: (j, 0, 0)),
             ),
         ),
-        compiler_params=pltpu.CompilerParams(vmem_limit_bytes=32 * 1024 * 1024),
+        compiler_params=pltpu.CompilerParams(vmem_limit_bytes=60 * 1024 * 1024),
         name="finish",
     )(home, back_a, back_b, normed, projected, one, two)
 

time: 267 us -> 258 us (0.966)
  local copies, waits for them, and re-layouts: 7.11 us -> 0 us
    unnamed x14 -> x0, local copies, waits for them, and re-layouts: 7.11 us -> none
    pallas_call x1, Pallas kernels: 141 us -> 135 us  [leave(): pl.pallas_call(functools.partial(leave_body, shards, owners), out_shape=(...]
    pallas_call x1, Pallas kernels: 6.75 us -> 11.1 us  [finish(): pl.pallas_call(finish_body, out_shape=(jax.ShapeDtypeStruct((slots, 2 * c...]
where the time goes in v5:
time: 258 us
  Pallas kernels  257 us (100%)
    pallas_call x1, Pallas kernels, leave(): pl.pallas_call(functools.partial(leave_body, shards, owners), out_shape=(...  135 us
    pallas_call x1, Pallas kernels, enter(): pl.pallas_call(functools.partial(enter_body, shards, owners), out_shape=(...  107 us
    pallas_call x1, Pallas kernels, finish(): pl.pallas_call(finish_body, out_shape=(jax.ShapeDtypeStruct((slots, 2 * c...  11.1 us

profile of v5, /device:TPU:1, one launch (start us, length us, event | category | flops | bytes accessed | tf_op | source)
XLA Modules:
  0.0 257.5 jit_solution(5952870546788798328)
XLA Ops:
  0.6 106.9 %enter.1 = (bf16[8,256,768]{2,1,0:T(8,128)(2,1)}, bf16[8,256,768]{2,1,0:T(8,128)(2,1)}, bf16[768,768]{1,0:T(8,128)(2,1)}, bf16[768,768]{1,0:T(8,128)(2,1)}, f32[768,256]{1,0:T(8,128)}, /*index=5*/f32[8,256,256]{2,1,0:T(8,128)}) custom-call(s32[128]{0:T(128)} %table.5, f32[8,256,768]{2,1,0:T(8,128)} %g_ref.1, f32[8,256,256]{2,1,0:T(8,128)} %b_ref.1), custom_call_target="tpu_custom_call" | custom-call | tf_op jit(solution)/shard_map/enter/pallas_call | solution.py:272
  107.5 3.3 %refresh.1 = (bf16[768,256]{1,0:T(8,128)(2,1)}, bf16[768,256]{1,0:T(8,128)(2,1)}, f32[8,32,768]{2,1,0:T(8,128)}, f32[1]{0:T(128)}, s32[8]{0:T(128)}) custom-call(s32[128]{0:T(128)} %table.5, s32[128]{0:T(128)} %cost.1, bf16[768,768]{1,0:T(8,128)(2,1)} %get-tuple-element.19.kh_ref, bf16[768,768]{1,0:T(8,128)(2,1)} %get-tuple-element.20.kl_ref, ...), custom_call_target="tpu_custom_call" | custom-call | tf_op jit(solution)/shard_map/refresh/pallas_call | solution.py:339
  110.8 135.5 %leave.1 = (f32[16,128,256]{2,1,0:T(8,128)}, f32[16,128,256]{2,1,0:T(8,128)}, f32[8,8,32,768]{3,2,1,0:T(8,128)}, f32[8,32,768]{2,1,0:T(8,128)}) custom-call(s32[128]{0:T(128)} %table.5, f32[1]{0:T(128)} %get-tuple-element.23.keep_ref, bf16[768,256]{1,0:T(8,128)(2,1)} %get-tuple-element.24.mh_ref, bf16[768,256]{1,0:T(8,128)(2,1)} %get-tuple-element.25.ml_ref, ...), custom_call_target="tpu_custom_call" | custom-call | tf_op jit(solution)/shard_map/leave/pallas_call | solution.py:518
  246.3 11.1 %finish.1 = (f32[8,256,256]{2,1,0:T(8,128)}, f32[8,32,768]{2,1,0:T(8,128)}, f32[8,32,768]{2,1,0:T(8,128)}, bf16[8,256,768]{2,1,0:T(8,128)(2,1)}) custom-call(s32[8]{0:T(128)} %get-tuple-element.22.home_ref, f32[16,128,256]{2,1,0:T(8,128)} %get-tuple-element.30.back_a, f32[16,128,256]{2,1,0:T(8,128)} %get-tuple-element.31.back_b, ...), custom_call_target="tpu_custom_call" | custom-call | tf_op jit(solution)/shard_map/finish/pallas_call | solution.py:560

commit v6 on v5

--- a/solution.py
+++ b/solution.py
@@ -143,11 +143,13 @@
     return found
 
 
-def enter_body(shards, owners, table, g_ref, b_ref, gh_out, gl_out, kh_out, kl_out, z_out, p_out,
-               gland, gh, gl, kacc, kh, kl, stage, landed, stage2, pland,
-               g_send, g_recv, a_send, a_recv, b_send, b_recv, own_sem, h_sem, l_sem, p_sem, k_sem):
+def enter_body(shards, owners, table, g_ref, b_hbm, gh_out, gl_out, kh_out, kl_out, z_out, p_out,
+               b_ref, gland, gh, gl, kacc, kh, kl, stage, landed, stage2, pland,
+               g_send, g_recv, a_send, a_recv, b_send, b_recv, own_sem, in_sem, h_sem, l_sem, p_sem, k_sem):
     s_me = lax.axis_index("shard")
     o_me = lax.axis_index("owner")
+    load = pltpu.make_async_copy(b_hbm, b_ref, in_sem)
+    load.start()
     greet((("shard", shards), ("owner", owners)))
     slots = shards
 
@@ -165,6 +167,7 @@
         t = at_shard(d)
         remote(g_ref.at[t], gland.at[s_me], g_send.at[d], g_recv.at[d], "shard", t).start()
 
+    load.wait()
     for k, t, _ in partners(o_me):
         stage[t] = b_ref[slot_at(table, o_me, slots, t)]
         remote(stage.at[t], landed.at[o_me], a_send.at[k], a_recv.at[k], "owner", t).start()
@@ -234,7 +237,7 @@
 
     def project(f):
         pltpu.make_async_copy(pland.at[f], p_out.at[f], p_sem.at[f]).start()
-        return dot3((gh[f], gl[f]), split(pland[f]), TN)
+        return dot3(split(pland[f]), (gh[f], gl[f]), TN)
 
     z_out[...] = project(s_me)
 
@@ -276,16 +279,16 @@
             jax.ShapeDtypeStruct((shards, rows, cols), BF),
             jax.ShapeDtypeStruct((cols, cols), BF),
             jax.ShapeDtypeStruct((cols, cols), BF),
-            jax.ShapeDtypeStruct((cols, rank), F32),
+            jax.ShapeDtypeStruct((rank, cols), F32),
             jax.ShapeDtypeStruct((shards, rows, rank), F32),
         ),
-        in_specs=[smem, hbm, vmem],
+        in_specs=[smem, hbm, hbm],
         out_specs=(hbm, hbm, hbm, hbm, vmem, hbm),
         scratch_shapes=[
-            V((shards, rows, cols), F32), V((shards, rows, cols), BF), V((shards, rows, cols), BF), V((cols, cols), F32), V((cols, cols), BF), V((cols, cols), BF),
+            V((shards, rows, rank), F32), V((shards, rows, cols), F32), V((shards, rows, cols), BF), V((shards, rows, cols), BF), V((cols, cols), F32), V((cols, cols), BF), V((cols, cols), BF),
             V((owners, rows, rank), F32), V((owners, rows, rank), F32), V((shards, rows, rank), F32), V((shards, rows, rank), F32),
             sem((shards,)), sem((shards,)), sem((owners,)), sem((owners,)), sem((shards,)), sem((shards,)),
-            sem, sem((shards,)), sem((shards,)), sem((shards,)), sem((2,)),
+            sem, sem, sem((shards,)), sem((shards,)), sem((shards,)), sem((2,)),
         ],
         compiler_params=pltpu.CompilerParams(
             collective_id=0, has_side_effects=True, vmem_limit_bytes=56 * 1024 * 1024
@@ -298,7 +301,6 @@
     s_me = lax.axis_index("shard")
     o_me = lax.axis_index("owner")
     shards, part, cols = pj_ref.shape
-    rank = zin_ref.shape[1]
     count = cost[o_me * shards + s_me]
     keep_ref[0] = jnp.where(count > 0, 0.0, 1.0)
     for j in range(shards):
@@ -308,16 +310,16 @@
     @pl.loop(0, count)
     def _(it):
         z = split(z_ref[...])
-        w_ref[...] = dot3((kh_ref[...], kl_ref[...]), z, NN)
+        w_ref[...] = dot3(z, (kh_ref[...], kl_ref[...]), NN)
         w = split(w_ref[...])
-        c_ref[...] = dot3(z, w, TN)
+        c_ref[...] = dot3(z, w, NT)
         factor(c_ref, xh, xl, ls, rs)
         x = (xh[...], xl[...])
-        z_ref[...] = dot3(w, x, NT)
+        z_ref[...] = dot3(x, w, NN)
 
         @pl.when(it == count - 1)
         def _():
-            h, l = split(dot3(z, x, NT))
+            h, l = split(dot3(x, z, NN))
             mh_ref[...] = h
             ml_ref[...] = l
 
@@ -326,21 +328,19 @@
         mh_ref[...] = jnp.zeros_like(mh_ref)
         ml_ref[...] = jnp.zeros_like(ml_ref)
 
-    for c in range(cols // 256):
-        t = z_ref[256 * c:256 * c + 256, :].T
-        for s in range(shards):
-            pj_ref[s, :, 256 * c:256 * c + 256] = t[part * s:part * s + part, :]
+    for s in range(shards):
+        pj_ref[s] = z_ref[part * s:part * s + part, :]
 
 
 def refresh(table, cost, shards, kh, kl, z):
-    cols, rank = z.shape
+    rank, cols = z.shape
     smem = pl.BlockSpec(memory_space=pltpu.SMEM)
     vmem = pl.BlockSpec(memory_space=V)
     return pl.pallas_call(
         body,
         out_shape=(
-            jax.ShapeDtypeStruct((cols, rank), BF),
-            jax.ShapeDtypeStruct((cols, rank), BF),
+            jax.ShapeDtypeStruct((rank, cols), BF),
+            jax.ShapeDtypeStruct((rank, cols), BF),
             jax.ShapeDtypeStruct((shards, rank // shards, cols), F32),
             jax.ShapeDtypeStruct((1,), F32),
             jax.ShapeDtypeStruct((shards,), jnp.int32),
@@ -348,7 +348,7 @@
         in_specs=[smem, smem, vmem, vmem, vmem],
         out_specs=(vmem, vmem, vmem, smem, smem),
         scratch_shapes=[
-            V((cols, rank), F32), V((cols, rank), F32), V((rank, rank), F32), V((rank, rank), BF), V((rank, rank), BF),
+            V((rank, cols), F32), V((rank, cols), F32), V((rank, rank), F32), V((rank, rank), BF), V((rank, rank), BF),
             V((3 * rank, rank), BF), V((3 * rank, 2 * rank), BF),
         ],
         compiler_params=pltpu.CompilerParams(vmem_limit_bytes=56 * 1024 * 1024),
@@ -371,13 +371,14 @@
 
 def leave_body(shards, owners, table, keep_ref, mh_ref, ml_ref, pj_ref, gh_hbm, gl_hbm, p_hbm, one_ref, two_ref,
                back_a, back_b, normed_out, proj_out,
-               gh, gl, p_in, pn, pj1, pj_stage, pj2, pn1a, pn1b, pn_stage, normed,
+               gh, gl, p_in, pn, pj1a, pj1b, pj_stage, pj2, pn1a, pn1b, pn_stage, normed,
                h_sem, l_sem, i_sem, j_send, j_recv, jo_send, jo_recv, p_send, p_recv, po_send, po_recv,
                n_send, n_recv, f_send, f_recv, own_sem):
     s_me = lax.axis_index("shard")
     o_me = lax.axis_index("owner")
     slots = one_ref.shape[0]
-    pn1, back = (pn1a, pn1b), (back_a, back_b)
+    pn1, back, pj1 = (pn1a, pn1b), (back_a, back_b), (pj1a, pj1b)
+    half = pj1a.shape[1]
     chunk = pn1a.shape[1]
 
     def at_shard(d):
@@ -403,19 +404,24 @@
 
     greet((("shard", shards), ("owner", owners)))
 
-    @pl.loop(1, shards)
-    def _(d):
-        t = at_shard(d)
-        remote(pj_ref.at[t], pj1.at[s_me], j_send.at[d], j_recv.at[d], "shard", t).start()
-
-    pj1[s_me] = pj_ref[s_me]
+    def part(q):
+        return slice(q * half, (q + 1) * half)
+
+    for q in range(2):
+
+        @pl.loop(1, shards)
+        def _(d):
+            t = at_shard(d)
+            remote(pj_ref.at[t, part(q)], pj1[q].at[s_me], j_send.at[q, d], j_recv.at[q, d], "shard", t).start()
+
+        pj1[q][s_me] = pj_ref[s_me, part(q)]
+
     keep = keep_ref[0]
 
     def basis_rows(t, c):
-        return dot3((gh[t, rows(c)], gl[t, rows(c)]), (mh_ref[...], ml_ref[...]), NN) + keep * p_in[t, rows(c)]
-
-    for c in range(CHUNKS):
-
+        return dot3((gh[t, rows(c)], gl[t, rows(c)]), (mh_ref[...], ml_ref[...]), NT) + keep * p_in[t, rows(c)]
+
+    def send_basis(c):
         @pl.loop(1, shards)
         def _(d):
             t = at_shard(d)
@@ -437,15 +443,23 @@
             found = jnp.where(lax.div(e, slots) == o_me, lax.rem(e, slots), found)
         return found
 
-    @pl.loop(1, shards)
-    def _(d):
-        remote(pj_ref.at[at_shard(d)], pj1.at[from_shard(d)], j_send.at[d], j_recv.at[d], "shard", at_shard(d)).wait()
-
-    for k, t, _ in partners(o_me):
-        pj_stage[t] = pj1[expert_at(t)]
-        remote(pj_stage.at[t], pj2.at[o_me], jo_send.at[k], jo_recv.at[k], "owner", t).start()
-
-    pj2[o_me] = pj1[expert_at(o_me)]
+    send_basis(0)
+    for q in range(2):
+
+        @pl.loop(1, shards)
+        def _(d):
+            t = at_shard(d)
+            remote(pj_ref.at[t, part(q)], pj1[q].at[from_shard(d)], j_send.at[q, d], j_recv.at[q, d], "shard", t).wait()
+
+        for k, t, _ in partners(o_me):
+            pj_stage[q, t] = pj1[q][expert_at(t)]
+            remote(pj_stage.at[q, t], pj2.at[q, o_me], jo_send.at[q, k], jo_recv.at[q, k], "owner", t).start()
+
+        pj2[q, o_me] = pj1[q][expert_at(o_me)]
+
+    for c in range(1, CHUNKS):
+        send_basis(c)
+
     own = []
     for c in range(CHUNKS):
 
@@ -462,12 +476,14 @@
         own.append(pltpu.make_async_copy(pn_stage.at[c, o_me], back[c].at[o_me], own_sem.at[c]))
         own[-1].start()
 
-    for k, t, source in partners(o_me):
-        remote(pj_stage.at[t], pj2.at[source], jo_send.at[k], jo_recv.at[k], "owner", t).wait()
+    for q in range(2):
+        for k, t, source in partners(o_me):
+            remote(pj_stage.at[q, t], pj2.at[q, source], jo_send.at[q, k], jo_recv.at[q, k], "owner", t).wait()
 
     @pl.loop(0, slots)
     def _(j):
-        projected = pj2[lax.div(table[o_me * slots + j], slots)]
+        home = lax.div(table[o_me * slots + j], slots)
+        projected = jnp.concatenate([pj2[0, home], pj2[1, home]], axis=0)
         proj_out[j] = projected
         one, two = adam(one_ref[j], two_ref[j], projected)
         normed[j] = one / (jnp.sqrt(two) + EPSILON)
@@ -527,11 +543,12 @@
         out_specs=(hbm, hbm, hbm, vmem),
         scratch_shapes=[
             V(gh.shape, BF), V(gh.shape, BF), V(p.shape, F32), V((CHUNKS, shards, chunk, rank), F32),
-            V((shards, part, cols), F32), V((owners, part, cols), F32), V((owners, part, cols), F32),
+            V((shards, part // 2, cols), F32), V((shards, part // 2, cols), F32),
+            V((2, owners, part // 2, cols), F32), V((2, owners, part // 2, cols), F32),
             V((shards, chunk, rank), F32), V((shards, chunk, rank), F32), V((CHUNKS, owners, chunk, rank), F32),
             V((slots, part, cols), F32),
             dma((shards,)), dma((shards,)), dma((shards,)),
-            dma((shards,)), dma((shards,)), dma((owners,)), dma((owners,)),
+            dma((2, shards)), dma((2, shards)), dma((2, owners)), dma((2, owners)),
             dma((CHUNKS, shards)), dma((CHUNKS, shards)), dma((CHUNKS, owners)), dma((CHUNKS, owners)),
             dma((shards // 2,)), dma((shards // 2,)), dma((shards // 2,)), dma((shards // 2,)), dma((CHUNKS + 1,)),
         ],
@@ -542,21 +559,74 @@
     )(table, keep, mh, ml, pj, gh, gl, p, one, two)
 
 
-def finish_body(home_ref, back_a, back_b, normed_ref, proj_ref, one_ref, two_ref, basis_out, one_out, two_out, update_out):
-    one_out[0], two_out[0] = adam(one_ref[0], two_ref[0], proj_ref[0])
-    shards, _, part, cols = normed_ref.shape
-    normed = split(normed_ref[:, 0].reshape(shards * part, cols))
-    chunk = back_a.shape[1]
-    for c, ref in enumerate((back_a, back_b)):
-        at = slice(c * chunk, (c + 1) * chunk)
-        basis_out[0, at] = ref[0]
-        update_out[0, at] = (GALORE_SCALE * dot3(split(ref[0]), normed, NN)).astype(BF)
+def finish_body(home_ref, back_a, back_b, normed_ref, proj_ref, one_ref, two_ref, basis_out, one_out, two_out, update_out,
+                basis, normed, proj, one, two, update, b_sem, n_sem, m_sem, bo_sem, u_sem, mo_sem):
+    slots, rows, _ = basis.shape
+    chunk = rows // 2
+    shards, part, cols = normed.shape[1:]
+
+    def halves(j):
+        return [
+            pltpu.make_async_copy(ref.at[home_ref[j]], basis.at[j, c * chunk:(c + 1) * chunk], b_sem.at[c, j])
+            for c, ref in enumerate((back_a, back_b))
+        ]
+
+    def step(j):
+        return pltpu.make_async_copy(normed_ref.at[:, j], normed.at[j], n_sem.at[j])
+
+    def basis_save(j):
+        return pltpu.make_async_copy(basis.at[j], basis_out.at[j], bo_sem.at[j])
+
+    def update_save(j):
+        return pltpu.make_async_copy(update.at[j], update_out.at[j], u_sem.at[j])
+
+    moments = [
+        pltpu.make_async_copy(src, dst, m_sem.at[k])
+        for k, (src, dst) in enumerate(((proj_ref, proj), (one_ref, one), (two_ref, two)))
+    ]
+
+    @pl.loop(0, slots)
+    def _(j):
+        for copy in halves(j):
+            copy.start()
+        step(j).start()
+
+    for copy in moments:
+        copy.start()
+
+    @pl.loop(0, slots)
+    def _(j):
+        for copy in halves(j):
+            copy.wait()
+        basis_save(j).start()
+        step(j).wait()
+        product = dot3(split(basis[j]), split(normed[j].reshape(shards * part, cols)), NN)
+        update[j] = (GALORE_SCALE * product).astype(BF)
+        update_save(j).start()
+
+    for copy in moments:
+        copy.wait()
+    one[...], two[...] = adam(one[...], two[...], proj[...])
+    saves = [
+        pltpu.make_async_copy(src, dst, mo_sem.at[k]) for k, (src, dst) in enumerate(((one, one_out), (two, two_out)))
+    ]
+    for copy in saves:
+        copy.start()
+
+    @pl.loop(0, slots)
+    def _(j):
+        basis_save(j).wait()
+        update_save(j).wait()
+
+    for copy in saves:
+        copy.wait()
 
 
 def finish(home, back_a, back_b, normed, projected, one, two):
     shards, slots, part, cols = normed.shape
     _, chunk, rank = back_a.shape
-    small = pl.BlockSpec((1, part, cols), lambda j, home: (j, 0, 0))
+    dma = pltpu.SemaphoreType.DMA
+    hbm = pl.BlockSpec(memory_space=pl.ANY)
     return pl.pallas_call(
         finish_body,
         out_shape=(
@@ -565,21 +635,13 @@
             jax.ShapeDtypeStruct(two.shape, F32),
             jax.ShapeDtypeStruct((slots, 2 * chunk, cols), BF),
         ),
-        grid_spec=pltpu.PrefetchScalarGridSpec(
-            num_scalar_prefetch=1,
-            grid=(slots,),
-            in_specs=[
-                pl.BlockSpec((1, chunk, rank), lambda j, home: (home[j], 0, 0)),
-                pl.BlockSpec((1, chunk, rank), lambda j, home: (home[j], 0, 0)),
-                pl.BlockSpec((shards, 1, part, cols), lambda j, home: (0, j, 0, 0)),
-                small, small, small,
-            ],
-            out_specs=(
-                pl.BlockSpec((1, 2 * chunk, rank), lambda j, home: (j, 0, 0)),
-                small, small,
-                pl.BlockSpec((1, 2 * chunk, cols), lambda j, home: (j, 0, 0)),
-            ),
-        ),
+        in_specs=[pl.BlockSpec(memory_space=pltpu.SMEM)] + [hbm] * 6,
+        out_specs=(hbm,) * 4,
+        scratch_shapes=[
+            V((slots, 2 * chunk, rank), F32), V((slots, shards, part, cols), F32),
+            V(one.shape, F32), V(one.shape, F32), V(one.shape, F32), V((slots, 2 * chunk, cols), BF),
+            dma((2, slots)), dma((slots,)), dma((3,)), dma((slots,)), dma((slots,)), dma((2,)),
+        ],
         compiler_params=pltpu.CompilerParams(vmem_limit_bytes=60 * 1024 * 1024),
         name="finish",
     )(home, back_a, back_b, normed, projected, one, two)

time: 258 us -> 253 us (0.981)
  Pallas kernels: 257 us -> 250 us
    pallas_call x1, Pallas kernels: 135 us -> 123 us  [leave(): pl.pallas_call(functools.partial(leave_body, shards, owners), out_shape=(...]
    pallas_call x1, Pallas kernels: 3.3 us -> 12.6 us  [refresh(): pl.pallas_call(body, out_shape=(jax.ShapeDtypeStruct((rank, cols), BF), j...]
    pallas_call x1, Pallas kernels: 11.1 us -> 7.94 us  [finish(): pl.pallas_call(finish_body, out_shape=(jax.ShapeDtypeStruct((slots, 2 * c...]
where the time goes in v6:
time: 253 us; the launch traced here: 250 us
  Pallas kernels  250 us (99%)
    pallas_call x1, Pallas kernels, leave(): pl.pallas_call(functools.partial(leave_body, shards, owners), out_shape=(...  123 us
    pallas_call x1, Pallas kernels, enter(): pl.pallas_call(functools.partial(enter_body, shards, owners), out_shape=(...  106 us
    pallas_call x1, Pallas kernels, refresh(): pl.pallas_call(body, out_shape=(jax.ShapeDtypeStruct((rank, cols), BF), j...  12.6 us
    pallas_call x1, Pallas kernels, finish(): pl.pallas_call(finish_body, out_shape=(jax.ShapeDtypeStruct((slots, 2 * c...  7.94 us

profile of v6, /device:TPU:1, one launch (start us, length us, event | category | flops | bytes accessed | tf_op | source)
XLA Modules:
  0.0 250.5 jit_solution(2088868345174627941)
XLA Ops:
  0.6 105.9 %enter.1 = (bf16[8,256,768]{2,1,0:T(8,128)(2,1)}, bf16[8,256,768]{2,1,0:T(8,128)(2,1)}, bf16[768,768]{1,0:T(8,128)(2,1)}, bf16[768,768]{1,0:T(8,128)(2,1)}, f32[256,768]{1,0:T(8,128)}, /*index=5*/f32[8,256,256]{2,1,0:T(8,128)}) custom-call(s32[128]{0:T(128)} %table.5, f32[8,256,768]{2,1,0:T(8,128)} %g_ref.1, f32[8,256,256]{2,1,0:T(8,128)} %b_hbm.1), custom_call_target="tpu_custom_call" | custom-call | tf_op jit(solution)/shard_map/enter/pallas_call | solution.py:275
  106.6 12.6 %refresh.1 = (bf16[256,768]{1,0:T(8,128)(2,1)}, bf16[256,768]{1,0:T(8,128)(2,1)}, f32[8,32,768]{2,1,0:T(8,128)}, f32[1]{0:T(128)}, s32[8]{0:T(128)}) custom-call(s32[128]{0:T(128)} %table.5, s32[128]{0:T(128)} %cost.1, bf16[768,768]{1,0:T(8,128)(2,1)} %get-tuple-element.19.kh_ref, bf16[768,768]{1,0:T(8,128)(2,1)} %get-tuple-element.20.kl_ref, ...), custom_call_target="tpu_custom_call" | custom-call | tf_op jit(solution)/shard_map/refresh/pallas_call | solution.py:339
  119.2 123.2 %leave.1 = (f32[16,128,256]{2,1,0:T(8,128)}, f32[16,128,256]{2,1,0:T(8,128)}, f32[8,8,32,768]{3,2,1,0:T(8,128)}, f32[8,32,768]{2,1,0:T(8,128)}) custom-call(s32[128]{0:T(128)} %table.5, f32[1]{0:T(128)} %get-tuple-element.23.keep_ref, bf16[256,768]{1,0:T(8,128)(2,1)} %get-tuple-element.24.mh_ref, bf16[256,768]{1,0:T(8,128)(2,1)} %get-tuple-element.25.ml_ref, ...), custom_call_target="tpu_custom_call" | custom-call | tf_op jit(solution)/shard_map/leave/pallas_call | solution.py:534
  242.4 7.9 %finish.1 = (f32[8,256,256]{2,1,0:T(8,128)}, f32[8,32,768]{2,1,0:T(8,128)}, f32[8,32,768]{2,1,0:T(8,128)}, bf16[8,256,768]{2,1,0:T(8,128)(2,1)}) custom-call(s32[8]{0:T(128)} %get-tuple-element.22.home_ref, f32[16,128,256]{2,1,0:T(8,128)} %get-tuple-element.30.back_a, f32[16,128,256]{2,1,0:T(8,128)} %get-tuple-element.31.back_b, ...), custom_call_target="tpu_custom_call" | custom-call | tf_op jit(solution)/shard_map/finish/pallas_call | solution.py:630

commit v7 on v6

--- a/solution.py
+++ b/solution.py
@@ -30,6 +30,7 @@
 def factor(c_ref, xh, xl, ls, rs):
     nb, sub_nb = PANEL, GROUP
     n = c_ref.shape[0]
+    tile = lax.broadcasted_iota(jnp.int32, (8, 128), 0)
     for p in range(n // nb):
         lo = p * nb
         need = [h for h in range(4) if (h < 2 and h * 128 + 128 > lo) or (h >= 2 and (h - 2) * 128 < lo + nb)]
@@ -57,21 +58,24 @@
         done = []
         for g in range(nb // sub_nb):
             b = g * sub_nb
-            rows = nb - b
-            rsub = lax.broadcasted_iota(jnp.int32, (rows, 128), 0)
-            cols = [jnp.broadcast_to(s[hd][:, off + b + k:off + b + k + 1], (rows, 128)) for k in range(sub_nb)]
+            cols = [jnp.broadcast_to(s[hd][:, off + b + k:off + b + k + 1], (nb - b, 128)) for k in range(sub_nb)]
             for j in range(sub_nb):
-                d = cols[j][j:j + 1, :]
-                r = 1.0 / d
+                jj = j % 8
+                d = cols[j][jj:jj + 1, :]
                 pivots.append(d)
-                m = jnp.where(rsub > j, cols[j] * r, 0.0)
+                m = cols[j] * (1.0 / d)
                 for k in range(j + 1, sub_nb):
-                    cols[k] = cols[k] - m * cols[k][j:j + 1, :]
+                    cols[k] = cols[k] - m * cols[k][jj:jj + 1, :]
+                low = jnp.where(tile > jj, m[0:8], 0.0)
+                if m.shape[0] > 8:
+                    low = jnp.concatenate([low, m[8:]], axis=0)
                 for h in need:
-                    s[h] = s[h] - m * s[h][j:j + 1, :]
-            done.append({h: s[h][0:sub_nb] for h in need})
-            if rows > sub_nb:
-                s = {h: s[h][sub_nb:] for h in need}
+                    s[h] = s[h] - low * s[h][jj:jj + 1, :]
+                if jj == 7:
+                    done.append({h: s[h][0:8] for h in need})
+                    if m.shape[0] > 8:
+                        s = {h: s[h][8:] for h in need}
+                        cols = [t[8:] for t in cols]
         scale = lax.rsqrt(jnp.concatenate(pivots, axis=0))
         for h in range(4):
             if h not in need:
@@ -369,11 +373,11 @@
     return one, two
 
 
-def leave_body(shards, owners, table, keep_ref, mh_ref, ml_ref, pj_ref, gh_hbm, gl_hbm, p_hbm, one_ref, two_ref,
+def leave_body(shards, owners, table, keep_ref, mh_ref, ml_ref, pj_ref, gh_hbm, gl_hbm, p_hbm, one_hbm, two_hbm,
                back_a, back_b, normed_out, proj_out,
-               gh, gl, p_in, pn, pj1a, pj1b, pj_stage, pj2, pn1a, pn1b, pn_stage, normed,
+               one_ref, two_ref, gh, gl, p_in, pn, pj1a, pj1b, pj_stage, pj2, pn1a, pn1b, pn_stage, normed,
                h_sem, l_sem, i_sem, j_send, j_recv, jo_send, jo_recv, p_send, p_recv, po_send, po_recv,
-               n_send, n_recv, f_send, f_recv, own_sem):
+               n_send, n_recv, f_send, f_recv, own_sem, m_sem):
     s_me = lax.axis_index("shard")
     o_me = lax.axis_index("owner")
     slots = one_ref.shape[0]
@@ -402,6 +406,9 @@
         for copy in loads(at_shard(d)):
             copy.start()
 
+    moments = (pltpu.make_async_copy(one_hbm, one_ref, m_sem.at[0]), pltpu.make_async_copy(two_hbm, two_ref, m_sem.at[1]))
+    for copy in moments:
+        copy.start()
     greet((("shard", shards), ("owner", owners)))
 
     def part(q):
@@ -414,7 +421,7 @@
             t = at_shard(d)
             remote(pj_ref.at[t, part(q)], pj1[q].at[s_me], j_send.at[q, d], j_recv.at[q, d], "shard", t).start()
 
-        pj1[q][s_me] = pj_ref[s_me, part(q)]
+        pltpu.make_async_copy(pj_ref.at[s_me, part(q)], pj1[q].at[s_me], m_sem.at[2 + q]).start()
 
     keep = keep_ref[0]
 
@@ -443,7 +450,6 @@
             found = jnp.where(lax.div(e, slots) == o_me, lax.rem(e, slots), found)
         return found
 
-    send_basis(0)
     for q in range(2):
 
         @pl.loop(1, shards)
@@ -451,17 +457,19 @@
             t = at_shard(d)
             remote(pj_ref.at[t, part(q)], pj1[q].at[from_shard(d)], j_send.at[q, d], j_recv.at[q, d], "shard", t).wait()
 
+        pltpu.make_async_copy(pj_ref.at[s_me, part(q)], pj1[q].at[s_me], m_sem.at[2 + q]).wait()
         for k, t, _ in partners(o_me):
             pj_stage[q, t] = pj1[q][expert_at(t)]
             remote(pj_stage.at[q, t], pj2.at[q, o_me], jo_send.at[q, k], jo_recv.at[q, k], "owner", t).start()
 
         pj2[q, o_me] = pj1[q][expert_at(o_me)]
 
-    for c in range(1, CHUNKS):
+    for c in range(0, CHUNKS):
         send_basis(c)
 
     own = []
-    for c in range(CHUNKS):
+
+    def pass_basis(c):
 
         @pl.loop(1, shards)
         def _(d):
@@ -476,9 +484,15 @@
         own.append(pltpu.make_async_copy(pn_stage.at[c, o_me], back[c].at[o_me], own_sem.at[c]))
         own[-1].start()
 
+    for c in range(CHUNKS):
+        pass_basis(c)
+
     for q in range(2):
         for k, t, source in partners(o_me):
             remote(pj_stage.at[q, t], pj2.at[q, source], jo_send.at[q, k], jo_recv.at[q, k], "owner", t).wait()
+
+    for copy in moments:
+        copy.wait()
 
     @pl.loop(0, slots)
     def _(j):
@@ -539,10 +553,10 @@
             jax.ShapeDtypeStruct((shards, slots, part, cols), F32),
             jax.ShapeDtypeStruct((slots, part, cols), F32),
         ),
-        in_specs=[smem, smem, vmem, vmem, vmem, hbm, hbm, hbm, vmem, vmem],
+        in_specs=[smem, smem, vmem, vmem] + [hbm] * 6,
         out_specs=(hbm, hbm, hbm, vmem),
         scratch_shapes=[
-            V(gh.shape, BF), V(gh.shape, BF), V(p.shape, F32), V((CHUNKS, shards, chunk, rank), F32),
+            V(one.shape, F32), V(two.shape, F32), V(gh.shape, BF), V(gh.shape, BF), V(p.shape, F32), V((CHUNKS, shards, chunk, rank), F32),
             V((shards, part // 2, cols), F32), V((shards, part // 2, cols), F32),
             V((2, owners, part // 2, cols), F32), V((2, owners, part // 2, cols), F32),
             V((shards, chunk, rank), F32), V((shards, chunk, rank), F32), V((CHUNKS, owners, chunk, rank), F32),
@@ -550,7 +564,7 @@
             dma((shards,)), dma((shards,)), dma((shards,)),
             dma((2, shards)), dma((2, shards)), dma((2, owners)), dma((2, owners)),
             dma((CHUNKS, shards)), dma((CHUNKS, shards)), dma((CHUNKS, owners)), dma((CHUNKS, owners)),
-            dma((shards // 2,)), dma((shards // 2,)), dma((shards // 2,)), dma((shards // 2,)), dma((CHUNKS + 1,)),
+            dma((shards // 2,)), dma((shards // 2,)), dma((shards // 2,)), dma((shards // 2,)), dma((CHUNKS + 1,)), dma((4,)),
         ],
         compiler_params=pltpu.CompilerParams(
             collective_id=1, has_side_effects=True, vmem_limit_bytes=56 * 1024 * 1024

time: 253 us -> 248 us (0.980)
  Pallas kernels: 250 us -> 245 us
    pallas_call x1, Pallas kernels: 123 us -> 119 us  [leave(): pl.pallas_call(functools.partial(leave_body, shards, owners), out_shape=(...]
where the time goes in v7:
time: 248 us; the launch traced here: 246 us
  Pallas kernels  245 us (99%)
    pallas_call x1, Pallas kernels, leave(): pl.pallas_call(functools.partial(leave_body, shards, owners), out_shape=(...  119 us
    pallas_call x1, Pallas kernels, enter(): pl.pallas_call(functools.partial(enter_body, shards, owners), out_shape=(...  106 us
    pallas_call x1, Pallas kernels, refresh(): pl.pallas_call(body, out_shape=(jax.ShapeDtypeStruct((rank, cols), BF), j...  12.5 us
    pallas_call x1, Pallas kernels, finish(): pl.pallas_call(finish_body, out_shape=(jax.ShapeDtypeStruct((slots, 2 * c...  7.94 us

profile of v7, /device:TPU:1, one launch (start us, length us, event | category | flops | bytes accessed | tf_op | source)
XLA Modules:
  0.0 245.9 jit_solution(16239172116021544134)
XLA Ops:
  0.6 105.9 %enter.1 = (bf16[8,256,768]{2,1,0:T(8,128)(2,1)}, bf16[8,256,768]{2,1,0:T(8,128)(2,1)}, bf16[768,768]{1,0:T(8,128)(2,1)}, bf16[768,768]{1,0:T(8,128)(2,1)}, f32[256,768]{1,0:T(8,128)}, /*index=5*/f32[8,256,256]{2,1,0:T(8,128)}) custom-call(s32[128]{0:T(128)} %table.5, f32[8,256,768]{2,1,0:T(8,128)} %g_ref.1, f32[8,256,256]{2,1,0:T(8,128)} %b_hbm.1), custom_call_target="tpu_custom_call" | custom-call | tf_op jit(solution)/shard_map/enter/pallas_call | solution.py:279
  106.6 12.5 %refresh.1 = (bf16[256,768]{1,0:T(8,128)(2,1)}, bf16[256,768]{1,0:T(8,128)(2,1)}, f32[8,32,768]{2,1,0:T(8,128)}, f32[1]{0:T(128)}, s32[8]{0:T(128)}) custom-call(s32[128]{0:T(128)} %table.5, s32[128]{0:T(128)} %cost.1, bf16[768,768]{1,0:T(8,128)(2,1)} %get-tuple-element.19.kh_ref, bf16[768,768]{1,0:T(8,128)(2,1)} %get-tuple-element.20.kl_ref, ...), custom_call_target="tpu_custom_call" | custom-call | tf_op jit(solution)/shard_map/refresh/pallas_call | solution.py:343
  119.1 118.6 %leave.1 = (f32[16,128,256]{2,1,0:T(8,128)}, f32[16,128,256]{2,1,0:T(8,128)}, f32[8,8,32,768]{3,2,1,0:T(8,128)}, f32[8,32,768]{2,1,0:T(8,128)}) custom-call(s32[128]{0:T(128)} %table.5, f32[1]{0:T(128)} %get-tuple-element.23.keep_ref, bf16[256,768]{1,0:T(8,128)(2,1)} %get-tuple-element.24.mh_ref, bf16[256,768]{1,0:T(8,128)(2,1)} %get-tuple-element.25.ml_ref, ...), custom_call_target="tpu_custom_call" | custom-call | tf_op jit(solution)/shard_map/leave/pallas_call | solution.py:548
  237.8 7.9 %finish.1 = (f32[8,256,256]{2,1,0:T(8,128)}, f32[8,32,768]{2,1,0:T(8,128)}, f32[8,32,768]{2,1,0:T(8,128)}, bf16[8,256,768]{2,1,0:T(8,128)(2,1)}) custom-call(s32[8]{0:T(128)} %get-tuple-element.22.home_ref, f32[16,128,256]{2,1,0:T(8,128)} %get-tuple-element.30.back_a, f32[16,128,256]{2,1,0:T(8,128)} %get-tuple-element.31.back_b, ...), custom_call_target="tpu_custom_call" | custom-call | tf_op jit(solution)/shard_map/finish/pallas_call | solution.py:644

commit v8 on v7

--- a/solution.py
+++ b/solution.py
@@ -121,7 +121,7 @@
 
 
 STEPS = (
-    (1, 1), (3, 3), (1, 3), (3, 1), (1, 0), (0, 1), (3, 0), (0, 3), (2, 0), (0, 2), (2, 2), (2, 1), (1, 2), (2, 3), (3, 2),
+    (2, 1), (1, 0), (0, 3), (1, 2), (3, 3), (3, 0), (2, 3), (0, 1), (1, 1), (3, 2), (1, 3), (2, 0), (3, 1), (0, 2), (2, 2),
 )
 SIDE = 4
 

time: 248 us -> 249 us (level)
    pallas_call x1, Pallas kernels: 119 us -> 130 us  [leave(): pl.pallas_call(functools.partial(leave_body, shards, owners), out_shape=(...]
    pallas_call x1, Pallas kernels: 12.5 us -> 3.29 us  [refresh(): pl.pallas_call(body, out_shape=(jax.ShapeDtypeStruct((rank, cols), BF), j...]
where the time goes in v8:
time: 249 us; the launch traced here: 248 us
  Pallas kernels  247 us (99%)
    pallas_call x1, Pallas kernels, leave(): pl.pallas_call(functools.partial(leave_body, shards, owners), out_shape=(...  130 us
    pallas_call x1, Pallas kernels, enter(): pl.pallas_call(functools.partial(enter_body, shards, owners), out_shape=(...  106 us
    pallas_call x1, Pallas kernels, finish(): pl.pallas_call(finish_body, out_shape=(jax.ShapeDtypeStruct((slots, 2 * c...  7.94 us

profile of v8, /device:TPU:1, one launch (start us, length us, event | category | flops | bytes accessed | tf_op | source)
XLA Modules:
  0.0 248.3 jit_solution(16162967880360065811)
XLA Ops:
  0.6 105.9 %enter.1 = (bf16[8,256,768]{2,1,0:T(8,128)(2,1)}, bf16[8,256,768]{2,1,0:T(8,128)(2,1)}, bf16[768,768]{1,0:T(8,128)(2,1)}, bf16[768,768]{1,0:T(8,128)(2,1)}, f32[256,768]{1,0:T(8,128)}, /*index=5*/f32[8,256,256]{2,1,0:T(8,128)}) custom-call(s32[128]{0:T(128)} %table.5, f32[8,256,768]{2,1,0:T(8,128)} %g_ref.1, f32[8,256,256]{2,1,0:T(8,128)} %b_hbm.1), custom_call_target="tpu_custom_call" | custom-call | tf_op jit(solution)/shard_map/enter/pallas_call | solution.py:279
  106.6 3.3 %refresh.1 = (bf16[256,768]{1,0:T(8,128)(2,1)}, bf16[256,768]{1,0:T(8,128)(2,1)}, f32[8,32,768]{2,1,0:T(8,128)}, f32[1]{0:T(128)}, s32[8]{0:T(128)}) custom-call(s32[128]{0:T(128)} %table.5, s32[128]{0:T(128)} %cost.1, bf16[768,768]{1,0:T(8,128)(2,1)} %get-tuple-element.19.kh_ref, bf16[768,768]{1,0:T(8,128)(2,1)} %get-tuple-element.20.kl_ref, ...), custom_call_target="tpu_custom_call" | custom-call | tf_op jit(solution)/shard_map/refresh/pallas_call | solution.py:343
  109.9 130.3 %leave.1 = (f32[16,128,256]{2,1,0:T(8,128)}, f32[16,128,256]{2,1,0:T(8,128)}, f32[8,8,32,768]{3,2,1,0:T(8,128)}, f32[8,32,768]{2,1,0:T(8,128)}) custom-call(s32[128]{0:T(128)} %table.5, f32[1]{0:T(128)} %get-tuple-element.23.keep_ref, bf16[256,768]{1,0:T(8,128)(2,1)} %get-tuple-element.24.mh_ref, bf16[256,768]{1,0:T(8,128)(2,1)} %get-tuple-element.25.ml_ref, ...), custom_call_target="tpu_custom_call" | custom-call | tf_op jit(solution)/shard_map/leave/pallas_call | solution.py:548
  240.2 7.9 %finish.1 = (f32[8,256,256]{2,1,0:T(8,128)}, f32[8,32,768]{2,1,0:T(8,128)}, f32[8,32,768]{2,1,0:T(8,128)}, bf16[8,256,768]{2,1,0:T(8,128)(2,1)}) custom-call(s32[8]{0:T(128)} %get-tuple-element.22.home_ref, f32[16,128,256]{2,1,0:T(8,128)} %get-tuple-element.30.back_a, f32[16,128,256]{2,1,0:T(8,128)} %get-tuple-element.31.back_b, ...), custom_call_target="tpu_custom_call" | custom-call | tf_op jit(solution)/shard_map/finish/pallas_call | solution.py:644

commit v9 on v8

--- a/solution.py
+++ b/solution.py
@@ -265,7 +265,7 @@
         copy.wait()
 
 
-EARLY = 5
+EARLY = 2
 
 
 def enter(table, gradient, basis):

time: 249 us -> 246 us (0.988)
  Pallas kernels: 247 us -> 244 us
    pallas_call x1, Pallas kernels: 130 us -> 118 us  [leave(): pl.pallas_call(functools.partial(leave_body, shards, owners), out_shape=(...]
    pallas_call x1, Pallas kernels: 3.29 us -> 12.5 us  [refresh(): pl.pallas_call(body, out_shape=(jax.ShapeDtypeStruct((rank, cols), BF), j...]
where the time goes in v9:
time: 246 us; the launch traced here: 245 us
  Pallas kernels  244 us (99%)
    pallas_call x1, Pallas kernels, leave(): pl.pallas_call(functools.partial(leave_body, shards, owners), out_shape=(...  118 us
    pallas_call x1, Pallas kernels, enter(): pl.pallas_call(functools.partial(enter_body, shards, owners), out_shape=(...  105 us
    pallas_call x1, Pallas kernels, refresh(): pl.pallas_call(body, out_shape=(jax.ShapeDtypeStruct((rank, cols), BF), j...  12.5 us
    pallas_call x1, Pallas kernels, finish(): pl.pallas_call(finish_body, out_shape=(jax.ShapeDtypeStruct((slots, 2 * c...  7.94 us

profile of v9, /device:TPU:1, one launch (start us, length us, event | category | flops | bytes accessed | tf_op | source)
XLA Modules:
  0.0 245.2 jit_solution(6638282414100711553)
XLA Ops:
  0.6 105.4 %enter.1 = (bf16[8,256,768]{2,1,0:T(8,128)(2,1)}, bf16[8,256,768]{2,1,0:T(8,128)(2,1)}, bf16[768,768]{1,0:T(8,128)(2,1)}, bf16[768,768]{1,0:T(8,128)(2,1)}, f32[256,768]{1,0:T(8,128)}, /*index=5*/f32[8,256,256]{2,1,0:T(8,128)}) custom-call(s32[128]{0:T(128)} %table.5, f32[8,256,768]{2,1,0:T(8,128)} %g_ref.1, f32[8,256,256]{2,1,0:T(8,128)} %b_hbm.1), custom_call_target="tpu_custom_call" | custom-call | tf_op jit(solution)/shard_map/enter/pallas_call | solution.py:279
  106.1 12.5 %refresh.1 = (bf16[256,768]{1,0:T(8,128)(2,1)}, bf16[256,768]{1,0:T(8,128)(2,1)}, f32[8,32,768]{2,1,0:T(8,128)}, f32[1]{0:T(128)}, s32[8]{0:T(128)}) custom-call(s32[128]{0:T(128)} %table.5, s32[128]{0:T(128)} %cost.1, bf16[768,768]{1,0:T(8,128)(2,1)} %get-tuple-element.19.kh_ref, bf16[768,768]{1,0:T(8,128)(2,1)} %get-tuple-element.20.kl_ref, ...), custom_call_target="tpu_custom_call" | custom-call | tf_op jit(solution)/shard_map/refresh/pallas_call | solution.py:343
  118.6 118.5 %leave.1 = (f32[16,128,256]{2,1,0:T(8,128)}, f32[16,128,256]{2,1,0:T(8,128)}, f32[8,8,32,768]{3,2,1,0:T(8,128)}, f32[8,32,768]{2,1,0:T(8,128)}) custom-call(s32[128]{0:T(128)} %table.5, f32[1]{0:T(128)} %get-tuple-element.23.keep_ref, bf16[256,768]{1,0:T(8,128)(2,1)} %get-tuple-element.24.mh_ref, bf16[256,768]{1,0:T(8,128)(2,1)} %get-tuple-element.25.ml_ref, ...), custom_call_target="tpu_custom_call" | custom-call | tf_op jit(solution)/shard_map/leave/pallas_call | solution.py:548
  237.1 7.9 %finish.1 = (f32[8,256,256]{2,1,0:T(8,128)}, f32[8,32,768]{2,1,0:T(8,128)}, f32[8,32,768]{2,1,0:T(8,128)}, bf16[8,256,768]{2,1,0:T(8,128)(2,1)}) custom-call(s32[8]{0:T(128)} %get-tuple-element.22.home_ref, f32[16,128,256]{2,1,0:T(8,128)} %get-tuple-element.30.back_a, f32[16,128,256]{2,1,0:T(8,128)} %get-tuple-element.31.back_b, ...), custom_call_target="tpu_custom_call" | custom-call | tf_op jit(solution)/shard_map/finish/pallas_call | solution.py:644

commit v10 on v9

--- a/solution.py
+++ b/solution.py
@@ -265,7 +265,7 @@
         copy.wait()
 
 
-EARLY = 2
+EARLY = 1
 
 
 def enter(table, gradient, basis):

time: 246 us -> 246 us (level)
    pallas_call x1, Pallas kernels: 118 us -> 128 us  [leave(): pl.pallas_call(functools.partial(leave_body, shards, owners), out_shape=(...]
    pallas_call x1, Pallas kernels: 12.5 us -> 3.29 us  [refresh(): pl.pallas_call(body, out_shape=(jax.ShapeDtypeStruct((rank, cols), BF), j...]
where the time goes in v10:
time: 246 us
  Pallas kernels  245 us (100%)
    pallas_call x1, Pallas kernels, leave(): pl.pallas_call(functools.partial(leave_body, shards, owners), out_shape=(...  128 us
    pallas_call x1, Pallas kernels, enter(): pl.pallas_call(functools.partial(enter_body, shards, owners), out_shape=(...  105 us
    pallas_call x1, Pallas kernels, finish(): pl.pallas_call(finish_body, out_shape=(jax.ShapeDtypeStruct((slots, 2 * c...  7.94 us

profile of v10, /device:TPU:1, one launch (start us, length us, event | category | flops | bytes accessed | tf_op | source)
XLA Modules:
  0.0 245.8 jit_solution(6931557351655064174)
XLA Ops:
  0.6 105.4 %enter.1 = (bf16[8,256,768]{2,1,0:T(8,128)(2,1)}, bf16[8,256,768]{2,1,0:T(8,128)(2,1)}, bf16[768,768]{1,0:T(8,128)(2,1)}, bf16[768,768]{1,0:T(8,128)(2,1)}, f32[256,768]{1,0:T(8,128)}, /*index=5*/f32[8,256,256]{2,1,0:T(8,128)}) custom-call(s32[128]{0:T(128)} %table.5, f32[8,256,768]{2,1,0:T(8,128)} %g_ref.1, f32[8,256,256]{2,1,0:T(8,128)} %b_hbm.1), custom_call_target="tpu_custom_call" | custom-call | tf_op jit(solution)/shard_map/enter/pallas_call | solution.py:279
  106.1 3.3 %refresh.1 = (bf16[256,768]{1,0:T(8,128)(2,1)}, bf16[256,768]{1,0:T(8,128)(2,1)}, f32[8,32,768]{2,1,0:T(8,128)}, f32[1]{0:T(128)}, s32[8]{0:T(128)}) custom-call(s32[128]{0:T(128)} %table.5, s32[128]{0:T(128)} %cost.1, bf16[768,768]{1,0:T(8,128)(2,1)} %get-tuple-element.19.kh_ref, bf16[768,768]{1,0:T(8,128)(2,1)} %get-tuple-element.20.kl_ref, ...), custom_call_target="tpu_custom_call" | custom-call | tf_op jit(solution)/shard_map/refresh/pallas_call | solution.py:343
  109.4 128.3 %leave.1 = (f32[16,128,256]{2,1,0:T(8,128)}, f32[16,128,256]{2,1,0:T(8,128)}, f32[8,8,32,768]{3,2,1,0:T(8,128)}, f32[8,32,768]{2,1,0:T(8,128)}) custom-call(s32[128]{0:T(128)} %table.5, f32[1]{0:T(128)} %get-tuple-element.23.keep_ref, bf16[256,768]{1,0:T(8,128)(2,1)} %get-tuple-element.24.mh_ref, bf16[256,768]{1,0:T(8,128)(2,1)} %get-tuple-element.25.ml_ref, ...), custom_call_target="tpu_custom_call" | custom-call | tf_op jit(solution)/shard_map/leave/pallas_call | solution.py:548
  237.7 7.9 %finish.1 = (f32[8,256,256]{2,1,0:T(8,128)}, f32[8,32,768]{2,1,0:T(8,128)}, f32[8,32,768]{2,1,0:T(8,128)}, bf16[8,256,768]{2,1,0:T(8,128)(2,1)}) custom-call(s32[8]{0:T(128)} %get-tuple-element.22.home_ref, f32[16,128,256]{2,1,0:T(8,128)} %get-tuple-element.30.back_a, f32[16,128,256]{2,1,0:T(8,128)} %get-tuple-element.31.back_b, ...), custom_call_target="tpu_custom_call" | custom-call | tf_op jit(solution)/shard_map/finish/pallas_call | solution.py:644
